TPU v7x, 256 devices: a whole 4x4x8 slice. The times are simulated.
256 devices in a mesh: dp: 16 (over z, core), ctx: 16 (over x, y).
Axes of the slice: x: 4, y: 4, z: 8, core: 2. Of those that a mesh axis runs over, the one named last changes fastest.
Arguments:
- qkv: bfloat16 [16, 2048, 12288], P('dp', 'ctx'), may hold values from -6 to 6
- segments: int32 [16, 2048], P('dp'), may hold values from 0 to 7, never falling along the last dimension, each value on 1 to 512 neighbouring positions
- short_taps: float32 [7, 12288], replicated, may hold values from -2.5 to 2.5
- long_taps: bfloat16 [128, 256], replicated, may hold values from -0.5 to 0.5
- cotangent: bfloat16 [16, 2048, 4096], P('dp', 'ctx'), may hold values from -8 to 8
Outputs:
- output: bfloat16 [16, 2048, 4096], P('dp', 'ctx')
- input_grad: bfloat16 [16, 2048, 12288], P('dp', 'ctx')
- short_grad: float32 [7, 12288], replicated
- long_grad: float32 [128, 256], replicated
Inputs may be any that keep to these rules, and one draw needn't show every extreme that they name: `segments`: within each pack the document numbers never fall; each of the 8 documents holds 1 to 512 positions, and one holds exactly that many.
All inputs are finite; a program needn't handle non-finite values.
Results may differ from a plain program's by a relative error of at most 0.0076.
Values may be sent and summed in bfloat16 or wider, within the bound.
A program may use at most 192 MiB of HBM per device.

v0:
```python
import jax
import jax.numpy as jnp
from jax import lax
from jax.sharding import PartitionSpec as P


def shifted_2(x, axis, by):
    length = lax.axis_size(axis)
    pairs = [(i, i + by) for i in range(length) if 0 <= i + by < length]
    return lax.ppermute(x, axis, pairs)


def banded(taps_row, rows):
    groups, taps_len = taps_row.shape
    span = rows + taps_len - 1
    padded = jnp.concatenate([taps_row, jnp.zeros((groups, rows), taps_row.dtype)], axis=1)
    tiled = jnp.tile(padded, (1, rows))[:, : rows * span]
    return tiled.reshape(groups, rows, span)


def block_marks(seg_ext, pack_index, first_row, rows, span, offset):
    marks = lax.dynamic_slice_in_dim(
        lax.dynamic_index_in_dim(seg_ext, pack_index, 0, False), first_row, span, 0
    )
    own_marks = marks[offset : offset + rows]
    return own_marks[:, None] == marks[None, :]


def long_apply(extended, seg_ext, band, offset, blocks):
    pack_count = extended.shape[0]
    groups, rows, span = band.shape
    channels = extended.shape[2]

    def one_block(block_index):
        pack_index = block_index // blocks
        first_row = block_index % blocks * rows
        block_rows = lax.dynamic_slice_in_dim(
            lax.dynamic_index_in_dim(extended, pack_index, 0, False), first_row, span, 0
        )
        allowed = block_marks(seg_ext, pack_index, first_row, rows, span, offset)
        matrix = jnp.where(allowed[None], band, jnp.zeros((), band.dtype))
        pieces = block_rows.reshape(span, groups, channels // groups)
        result = jnp.einsum("gpj,jgc->pgc", matrix, pieces, preferred_element_type=jnp.float32)
        return result.reshape(rows, channels)

    result = lax.map(one_block, jnp.arange(pack_count * blocks, dtype=jnp.int32))
    return result.reshape(pack_count, blocks * rows, channels)


def long_lags(left_all, extended, seg_ext, groups, taps_len, rows, blocks):
    pack_count = extended.shape[0]
    channels = extended.shape[2]
    span = rows + taps_len - 1
    row_ids = jnp.arange(rows, dtype=jnp.int32)[:, None, None]
    col_ids = jnp.arange(span, dtype=jnp.int32)[None, :, None]
    lag_ids = jnp.arange(taps_len, dtype=jnp.int32)[None, None, :]
    selector = (col_ids - row_ids == taps_len - 1 - lag_ids).astype(jnp.float32)

    def one_block(block_index):
        pack_index = block_index // blocks
        first_row = block_index % blocks * rows
        left_rows = lax.dynamic_slice_in_dim(
            lax.dynamic_index_in_dim(left_all, pack_index, 0, False), first_row, rows, 0
        )
        block_rows = lax.dynamic_slice_in_dim(
            lax.dynamic_index_in_dim(extended, pack_index, 0, False), first_row, span, 0
        )
        allowed = block_marks(seg_ext, pack_index, first_row, rows, span, taps_len - 1).astype(
            jnp.float32
        )
        weights = selector * allowed[:, :, None]
        left_parts = left_rows.reshape(rows, groups, channels // groups)
        right_parts = block_rows.reshape(span, groups, channels // groups)
        products = jnp.einsum(
            "pgc,jgc->gpj", left_parts, right_parts, preferred_element_type=jnp.float32
        )
        return jnp.einsum("gpj,pjt->tg", products, weights, precision=lax.Precision.HIGHEST)

    result = lax.map(one_block, jnp.arange(pack_count * blocks, dtype=jnp.int32))
    return jnp.sum(result, axis=0)


def short_forward(extended, seg_ext, short_taps):
    short_len = short_taps.shape[0]
    shard_rows = extended.shape[1] - short_len + 1
    own_marks = seg_ext[:, short_len - 1 :]
    running = jnp.zeros((extended.shape[0], shard_rows, extended.shape[2]), jnp.float32)
    for tap_index in range(short_len):
        source = short_len - 1 - tap_index
        matches = (seg_ext[:, source : source + shard_rows] == own_marks).astype(jnp.float32)[
            ..., None
        ]
        running = running + short_taps[tap_index] * (
            extended[:, source : source + shard_rows].astype(jnp.float32) * matches
        )
    return running


def short_backward(extended, seg_ext, short_taps):
    short_len = short_taps.shape[0]
    shard_rows = extended.shape[1] - short_len + 1
    own_marks = seg_ext[:, :shard_rows]
    running = jnp.zeros((extended.shape[0], shard_rows, extended.shape[2]), jnp.float32)
    for tap_index in range(short_len):
        matches = (seg_ext[:, tap_index : tap_index + shard_rows] == own_marks).astype(jnp.float32)[
            ..., None
        ]
        running = running + short_taps[tap_index] * (
            extended[:, tap_index : tap_index + shard_rows].astype(jnp.float32) * matches
        )
    return running


def short_terms(branch_grad, extended, seg_ext, short_len):
    shard_rows = branch_grad.shape[1]
    own_marks = seg_ext[:, short_len - 1 :]
    shifted = []
    for tap_index in range(short_len):
        source = short_len - 1 - tap_index
        matches = (seg_ext[:, source : source + shard_rows] == own_marks).astype(jnp.float32)[
            ..., None
        ]
        shifted.append(extended[:, source : source + shard_rows].astype(jnp.float32) * matches)
    stacked = jnp.stack(shifted, axis=0)
    return jnp.sum(branch_grad.astype(jnp.float32)[None] * stacked, axis=(1, 2))


def body(qkv, segments, short_taps, long_taps, cotangent):
    pack_count = qkv.shape[0]
    shard_rows = qkv.shape[1]
    taps_len = long_taps.shape[0]
    groups = long_taps.shape[1]
    short_len = short_taps.shape[0]
    channels = cotangent.shape[2]
    block_rows = min(16, taps_len)
    blocks = shard_rows // block_rows
    offset_row = lax.axis_index("ctx") * shard_rows
    padding = -jnp.ones((pack_count, taps_len - 1), jnp.int32)
    padded = jnp.concatenate([padding, segments, padding], axis=1)
    window = lax.dynamic_slice_in_dim(padded, offset_row, shard_rows + 2 * (taps_len - 1), 1)
    seg_fwd = window[:, : shard_rows + taps_len - 1]
    seg_bwd = window[:, taps_len - 1 :]
    seg_sfwd = window[:, taps_len - short_len : taps_len - 1 + shard_rows]
    seg_sbwd = window[:, taps_len - 1 : taps_len - 1 + shard_rows + short_len - 1]
    band_fwd = banded(long_taps.T[:, ::-1], block_rows)
    band_bwd = banded(long_taps.T, block_rows)
    before = shifted_2(qkv[:, shard_rows - short_len + 1 :], "ctx", 1)
    input_ext = jnp.concatenate([before, qkv], axis=1)
    short_out = short_forward(input_ext, seg_sfwd, short_taps).astype(jnp.bfloat16)
    query_part = short_out[..., :channels].astype(jnp.float32)
    key_rows = short_out[..., channels : 2 * channels].astype(jnp.float32)
    value_rows = short_out[..., 2 * channels :].astype(jnp.float32)
    product = (key_rows * value_rows).astype(jnp.bfloat16)
    earlier = shifted_2(product[:, shard_rows - taps_len + 1 :], "ctx", 1)
    product_ext = jnp.concatenate([earlier, product], axis=1)
    mixing = long_apply(product_ext, seg_fwd, band_fwd, taps_len - 1, blocks)
    output = (query_part * mixing).astype(jnp.bfloat16)
    upstream_f32 = cotangent.astype(jnp.float32)
    gate_grad = (upstream_f32 * query_part).astype(jnp.bfloat16)
    query_grad = upstream_f32 * mixing
    later = shifted_2(gate_grad[:, : taps_len - 1], "ctx", -1)
    grad_ext = jnp.concatenate([gate_grad, later], axis=1)
    product_grad = long_apply(grad_ext, seg_bwd, band_bwd, 0, blocks)
    branch_grad = jnp.concatenate(
        [query_grad, product_grad * value_rows, product_grad * key_rows], axis=2
    ).astype(jnp.bfloat16)
    after = shifted_2(branch_grad[:, : short_len - 1], "ctx", -1)
    branch_ext = jnp.concatenate([branch_grad, after], axis=1)
    input_grad = short_backward(branch_ext, seg_sbwd, short_taps).astype(jnp.bfloat16)
    short_sum = short_terms(branch_grad, input_ext, seg_sfwd, short_len)
    long_sum = long_lags(gate_grad, product_ext, seg_fwd, groups, taps_len, block_rows, blocks)
    short_total, long_total = lax.psum((short_sum, long_sum), ("dp", "ctx"))
    return (output, input_grad, short_total, long_total)


def solution(mesh):
    in_specs = (P("dp", "ctx", None), P("dp", None), P(), P(), P("dp", "ctx", None))
    out_specs = (P("dp", "ctx", None), P("dp", "ctx", None), P(), P())
    return jax.shard_map(body, mesh=mesh, in_specs=in_specs, out_specs=out_specs, check_vma=False)
```

profile of v0, /device:TPU:1, one launch (start us, length us, event | category | flops | bytes accessed | tf_op | source)
XLA Modules:
  0.0 784.6 jit_solution(7255184144404099007)
XLA Ops:
  8.9 4.0 collective-permute-start
  13.0 5.2 fusion.43
  22.7 4.6 copy.19
  31.5 4.4 copy.16
  35.9 8.8 %fusion.42 = bf16[1,128,12288]{2,1,0:T(8,128)(2,1)S(1)} fusion(bf16[1,128,12288]{2,1,0:T(8,128)(2,1)S(1)} %copy-done, bf16[1,6,12288]{2,1,0:T(8,128)(2,1)S(1)} %collective-permute-done, f32[128]{0:T(128)S(1)} %get-tuple-element.366, f32[12288]{0:T(1024)} %bitcast.153, f32[128]{0:T(128)S(1)} %get-tuple-element.367, f32[12288]{0:T(1024)} %bitcast.155, ...), kind=kLoop, calls=%fused_computation.56 | loop fusion | flops 70778880 | bytes 6786048 | tf_op jit(solution)/shard_map/convert_element_type | solution.py:149
  47.5 3.2 bitcast_dynamic-update-slice_fusion.5
  50.7 3.2 bitcast_dynamic-update-slice_fusion.4
  53.9 3.1 bitcast_dynamic-update-slice_fusion.3
  57.0 3.2 bitcast_dynamic-update-slice_fusion.2
  60.2 3.2 bitcast_dynamic-update-slice_fusion.1
  63.4 8.6 %collective-permute-done.2 = bf16[1,127,4096]{2,1,0:T(8,128)(2,1)S(1)} collective-permute-done((bf16[1,127,4096]{2,1,0:T(8,128)(2,1)}, bf16[1,127,4096]{2,1,0:T(8,128)(2,1)S(1)}, u32[]{:S(2)}, u32[]{:S(2)}) %collective-permute-start.2) | collective-permute-done | bytes 1040416 | tf_op jit(solution)/shard_map/ppermute | solution.py:10
  72.0 2.8 pad_maximum_fusion.4
  76.9 107.2 %while.38 = (s32[]{:T(128)}, f32[8,16,4096]{2,1,0:T(8,128)}, s32[8]{0:T(128)}, bf16[1,255,4096]{2,1,0:T(8,128)(2,1)}, s32[1,255]{1,0:T(1,128)S(1)}, /*index=5*/b...) while((s32[]{:T(128)}, f32[8,16,4096]{2,1,0:T(8,128)}, ...), condition=%wide.region_3.4_spmd, body=%wide.region_2.3_spmd.sunk | while | flops 19331328 | bytes 8346748 | solution.py:46
  83.8 3.6 fusion.93
  97.1 3.6 fusion.93
  110.6 3.6 fusion.93
  124.0 3.6 fusion.93
  137.4 3.6 fusion.93
  150.8 3.6 fusion.93
  164.1 3.6 fusion.93
  177.5 3.6 fusion.93
  184.0 4.3 fusion.52
  188.6 3.3 collective-permute-start.1
  191.9 3.6 bitcast_dynamic-update-slice_fusion
  195.5 16.9 %collective-permute-done.1 = bf16[1,127,4096]{2,1,0:T(8,128)(2,1)S(1)} collective-permute-done((bf16[1,127,4096]{2,1,0:T(8,128)(2,1)S(1)}, bf16[1,127,4096]{2,1,0:T(8,128)(2,1)S(1)}, u32[]{:S(2)}, u32[]{:S(2)}) %collective-permute-start.1) | collective-permute-done | bytes 1040416 | tf_op jit(solution)/shard_map/ppermute | solution.py:10
  214.0 3.3 copy.15
  218.8 98.4 %while.37 = (s32[]{:T(128)}, f32[8,16,4096]{2,1,0:T(8,128)}, s32[8]{0:T(128)S(1)}, bf16[1,255,4096]{1,2,0:T(8,128)(2,1)S(1)}, s32[1,255]{1,0:T(1,128)S(1)}, /*in...) while((s32[]{:T(128)}, f32[8,16,4096]{2,1,0:T(8,128)}, ...), condition=%wide.region_1.2_spmd, body=%wide.region_0.1_spmd.sunk | while | flops 19331328 | bytes 6003856 | solution.py:46
  221.4 2.4 constant_dynamic-slice_fusion.33
  224.0 4.3 fusion.89
  233.7 2.4 constant_dynamic-slice_fusion.33
  236.3 4.3 fusion.89
  246.0 2.4 constant_dynamic-slice_fusion.33
  248.6 4.3 fusion.89
  258.3 2.4 constant_dynamic-slice_fusion.33
  260.9 4.3 fusion.89
  270.6 2.4 constant_dynamic-slice_fusion.33
  273.2 4.3 fusion.89
  282.9 2.4 constant_dynamic-slice_fusion.33
  285.5 4.3 fusion.89
  297.8 4.3 fusion.89
  310.1 4.3 fusion.89
  317.2 3.8 fusion.53
  321.0 165.6 %while.39 = (s32[]{:T(128)}, f32[8,128,256]{2,1,0:T(8,128)}, s32[8]{0:T(128)S(1)}, s32[1,255]{1,0:T(1,128)S(1)}, bf16[1,128,4096]{2,1,0:T(8,128)(2,1)}, /*index=...) while((s32[]{:T(128)}, f32[8,128,256]{2,1,0:T(8,128)}, ...), condition=%wide.region_7.8_spmd.clone, body=%wide.region_6.7_spmd.clone.sunk | while | flops 919011840 | bytes 10868773 | solution.py:79
  327.7 4.6 fusion.98
  332.4 9.3 %fusion.100 = f32[8,128,256]{2,1,0:T(8,128)} fusion(f32[8,128,256]{2,1,0:T(8,128)} %get-tuple-element.589, s32[]{:T(128)} %get-tuple-element.588, f32[256,16,143]{2,1,0:T(8,128)} %fusion.98, s32[128]{0:T(128)S(1)} %get-tuple-element.610, s32[16,143]{1,0:T(8,128)S(1)} %get-tuple-element.611, f32[16,143]{1,0:T(8,128)S(1)} %compare_convert_fusion.14), kind=kOutput, calls=%fused_computation.28.clone.1 | convolution fusion | flops 900263936 | bytes 4344704 | tf_op jit(solution)/shard_map/while/body/eval_jaxpr/gpj,pjt->tg/dot_general | solution.py:77
  348.4 4.6 fusion.98
  353.1 9.3 %fusion.100 = f32[8,128,256]{2,1,0:T(8,128)} fusion(f32[8,128,256]{2,1,0:T(8,128)} %get-tuple-element.589, s32[]{:T(128)} %get-tuple-element.588, f32[256,16,143]{2,1,0:T(8,128)} %fusion.98, s32[128]{0:T(128)S(1)} %get-tuple-element.610, s32[16,143]{1,0:T(8,128)S(1)} %get-tuple-element.611, f32[16,143]{1,0:T(8,128)S(1)} %compare_convert_fusion.14), kind=kOutput, calls=%fused_computation.28.clone.1 | convolution fusion | flops 900263936 | bytes 4344704 | tf_op jit(solution)/shard_map/while/body/eval_jaxpr/gpj,pjt->tg/dot_general | solution.py:77
  369.0 4.6 fusion.98
  373.8 9.3 %fusion.100 = f32[8,128,256]{2,1,0:T(8,128)} fusion(f32[8,128,256]{2,1,0:T(8,128)} %get-tuple-element.589, s32[]{:T(128)} %get-tuple-element.588, f32[256,16,143]{2,1,0:T(8,128)} %fusion.98, s32[128]{0:T(128)S(1)} %get-tuple-element.610, s32[16,143]{1,0:T(8,128)S(1)} %get-tuple-element.611, f32[16,143]{1,0:T(8,128)S(1)} %compare_convert_fusion.14), kind=kOutput, calls=%fused_computation.28.clone.1 | convolution fusion | flops 900263936 | bytes 4344704 | tf_op jit(solution)/shard_map/while/body/eval_jaxpr/gpj,pjt->tg/dot_general | solution.py:77
  389.7 4.6 fusion.98
  394.5 9.2 %fusion.100 = f32[8,128,256]{2,1,0:T(8,128)} fusion(f32[8,128,256]{2,1,0:T(8,128)} %get-tuple-element.589, s32[]{:T(128)} %get-tuple-element.588, f32[256,16,143]{2,1,0:T(8,128)} %fusion.98, s32[128]{0:T(128)S(1)} %get-tuple-element.610, s32[16,143]{1,0:T(8,128)S(1)} %get-tuple-element.611, f32[16,143]{1,0:T(8,128)S(1)} %compare_convert_fusion.14), kind=kOutput, calls=%fused_computation.28.clone.1 | convolution fusion | flops 900263936 | bytes 4344704 | tf_op jit(solution)/shard_map/while/body/eval_jaxpr/gpj,pjt->tg/dot_general | solution.py:77
  410.4 4.6 fusion.98
  415.2 9.3 %fusion.100 = f32[8,128,256]{2,1,0:T(8,128)} fusion(f32[8,128,256]{2,1,0:T(8,128)} %get-tuple-element.589, s32[]{:T(128)} %get-tuple-element.588, f32[256,16,143]{2,1,0:T(8,128)} %fusion.98, s32[128]{0:T(128)S(1)} %get-tuple-element.610, s32[16,143]{1,0:T(8,128)S(1)} %get-tuple-element.611, f32[16,143]{1,0:T(8,128)S(1)} %compare_convert_fusion.14), kind=kOutput, calls=%fused_computation.28.clone.1 | convolution fusion | flops 900263936 | bytes 4344704 | tf_op jit(solution)/shard_map/while/body/eval_jaxpr/gpj,pjt->tg/dot_general | solution.py:77
  431.1 4.6 fusion.98
  435.9 9.3 %fusion.100 = f32[8,128,256]{2,1,0:T(8,128)} fusion(f32[8,128,256]{2,1,0:T(8,128)} %get-tuple-element.589, s32[]{:T(128)} %get-tuple-element.588, f32[256,16,143]{2,1,0:T(8,128)} %fusion.98, s32[128]{0:T(128)S(1)} %get-tuple-element.610, s32[16,143]{1,0:T(8,128)S(1)} %get-tuple-element.611, f32[16,143]{1,0:T(8,128)S(1)} %compare_convert_fusion.14), kind=kOutput, calls=%fused_computation.28.clone.1 | convolution fusion | flops 900263936 | bytes 4344704 | tf_op jit(solution)/shard_map/while/body/eval_jaxpr/gpj,pjt->tg/dot_general | solution.py:77
  451.8 4.6 fusion.98
  456.6 9.3 %fusion.100 = f32[8,128,256]{2,1,0:T(8,128)} fusion(f32[8,128,256]{2,1,0:T(8,128)} %get-tuple-element.589, s32[]{:T(128)} %get-tuple-element.588, f32[256,16,143]{2,1,0:T(8,128)} %fusion.98, s32[128]{0:T(128)S(1)} %get-tuple-element.610, s32[16,143]{1,0:T(8,128)S(1)} %get-tuple-element.611, f32[16,143]{1,0:T(8,128)S(1)} %compare_convert_fusion.14), kind=kOutput, calls=%fused_computation.28.clone.1 | convolution fusion | flops 900263936 | bytes 4344704 | tf_op jit(solution)/shard_map/while/body/eval_jaxpr/gpj,pjt->tg/dot_general | solution.py:77
  472.5 4.6 fusion.98
  477.3 9.3 %fusion.100 = f32[8,128,256]{2,1,0:T(8,128)} fusion(f32[8,128,256]{2,1,0:T(8,128)} %get-tuple-element.589, s32[]{:T(128)} %get-tuple-element.588, f32[256,16,143]{2,1,0:T(8,128)} %fusion.98, s32[128]{0:T(128)S(1)} %get-tuple-element.610, s32[16,143]{1,0:T(8,128)S(1)} %get-tuple-element.611, f32[16,143]{1,0:T(8,128)S(1)} %compare_convert_fusion.14), kind=kOutput, calls=%fused_computation.28.clone.1 | convolution fusion | flops 900263936 | bytes 4344704 | tf_op jit(solution)/shard_map/while/body/eval_jaxpr/gpj,pjt->tg/dot_general | solution.py:77
  490.9 3.2 maximum_convert_fusion
  494.2 18.4 %multiply_reduce_fusion = f32[7,12288]{1,0:T(8,128)} fusion(f32[7,1,128,12288]{3,2,1,0:T(8,128)} %bitcast_dynamic-update-slice_fusion, f32[128,12288]{1,0:T(8,128)} %maximum_convert_fusion), kind=kLoop, calls=%fused_computation.42 | loop fusion | flops 21934080 | bytes 50675712 | tf_op jit(solution)/shard_map/reduce_sum | solution.py:125
  514.7 3.2 pad_maximum_fusion
  518.0 9.7 %add_convert_fusion = bf16[1,128,12288]{2,1,0:T(8,128)(2,1)} fusion(bf16[1,134,12288]{2,1,0:T(8,128)(2,1)S(1)} %pad_maximum_fusion, f32[128]{0:T(128)S(1)} %copy-done.23, f32[128]{0:T(128)S(1)} %copy-done.20, f32[128]{0:T(128)S(1)} %copy-done.21, f32[128]{0:T(128)S(1)} %copy-done.22, f32[128]{0:T(128)S(1)} %copy-done.19, f32[128]{0:T(128)S(1)} %copy-done.24, ...), kind=kLoop, calls=%fused_computation.64 | loop fusion | flops 50331648 | bytes 25512960 | tf_op jit(solution)/shard_map/convert_element_type | solution.py:169
  527.7 246.7 %all-reduce.5.cloned.1.call-done = (f32[7,12288]{1,0:T(8,128)}, f32[128,256]{1,0:T(8,128)}) async-done(((f32[7,12288]{1,0:T(8,128)}, f32[128,256]{1,0:T(8,128)}), (f32[7,12288]{1,0:T(8,128)}, f32[128,256]{1,0:T(8,128)})) %all-reduce.5.cloned.1.call-update) | async-done | bytes 475152 | tf_op jit(solution)/shard_map/psum | solution.py:172
  (258 shorter events, 164.3 us)
Async XLA Ops:
  7.2 11.0 %copy-start.18 = (s32[1,2048]{1,0:T(1,128)S(1)}, s32[1,2048]{1,0:T(1,128)}, u32[]{:S(2)}) copy-start(s32[1,2048]{1,0:T(1,128)} %param.12) | copy-start | bytes 24580
  7.2 11.8 %copy-start.16 = (f32[7,12288]{1,0:T(8,128)S(1)}, f32[7,12288]{1,0:T(8,128)}, u32[]{:S(2)}) copy-start(f32[7,12288]{1,0:T(8,128)} %param.13) | copy-start | bytes 1032196
  7.2 13.4 %copy-start.17 = (bf16[128,256]{1,0:T(8,128)(2,1)S(1)}, bf16[128,256]{1,0:T(8,128)(2,1)}, u32[]{:S(2)}) copy-start(bf16[128,256]{1,0:T(8,128)(2,1)} %param.14) | copy-start | bytes 196612
  7.2 767.3 %all-reduce.5.cloned.1.call-start = ((), (), s32[]{:S(2)}) async-start(), calls=%async_computation | async-start | bytes 1048576 | tf_op jit(solution)/shard_map/psum | solution.py:172
  8.9 27.0 %collective-permute-start = (bf16[1,6,12288]{2,1,0:T(8,128)(2,1)}, bf16[1,6,12288]{2,1,0:T(8,128)(2,1)S(1)}, u32[]{:S(2)}, u32[]{:S(2)}) collective-permute-start(bf16[1,6,12288]{2,1,0:T(8,128)(2,1)} %slice.192), channel_id=1, source_target_pairs={{0,1},{1,2},{2,3},{3,4},{4,5},{5,6},{6,7},{7,8},{8,9},{9,10},{10,1... | collective-permute-start | bytes 442376 | tf_op jit(solution)/shard_map/ppermute | solution.py:10
  19.9 16.0 %copy-start.8 = (f32[1,12288]{1,0:T(1,128)}, f32[1,12288]{1,0:T(1,128)S(1)}, u32[]{:S(2)}) copy-start(f32[1,12288]{1,0:T(1,128)S(1)} %get-tuple-element.355) | copy-start | bytes 147460
  19.9 16.0 %copy-start.10 = (f32[1,12288]{1,0:T(1,128)}, f32[1,12288]{1,0:T(1,128)S(1)}, u32[]{:S(2)}) copy-start(f32[1,12288]{1,0:T(1,128)S(1)} %get-tuple-element.356) | copy-start | bytes 147460
  22.7 13.3 %copy-start = (bf16[1,128,12288]{2,1,0:T(8,128)(2,1)S(1)}, bf16[1,128,12288]{2,1,0:T(8,128)(2,1)}, u32[]{:S(2)}) copy-start(bf16[1,128,12288]{2,1,0:T(8,128)(2,1)} %param.11) | copy-start | bytes 9437188
  35.9 8.9 %copy-start.6 = (bf16[1,128,4096]{2,1,0:T(8,128)(2,1)S(1)}, bf16[1,128,4096]{2,1,0:T(8,128)(2,1)}, u32[]{:S(2)}) copy-start(bf16[1,128,4096]{2,1,0:T(8,128)(2,1)} %param.15) | copy-start | bytes 3145732
  44.8 5.9 copy-start.5
  46.2 25.8 %collective-permute-start.2 = (bf16[1,127,4096]{2,1,0:T(8,128)(2,1)}, bf16[1,127,4096]{2,1,0:T(8,128)(2,1)S(1)}, u32[]{:S(2)}, u32[]{:S(2)}) collective-permute-start(bf16[1,127,4096]{2,1,0:T(8,128)(2,1)} %bitcast.94), channel_id=1, source_target_pairs={{1,0},{2,1},{3,2},{4,3},{5,4},{6,5},{7,6},{8,7},{9,8},{10,9},{11,1... | collective-permute-start | bytes 3121160 | tf_op jit(solution)/shard_map/ppermute | solution.py:10
  184.0 7.8 copy-start.1
  188.6 23.8 %collective-permute-start.1 = (bf16[1,127,4096]{2,1,0:T(8,128)(2,1)S(1)}, bf16[1,127,4096]{2,1,0:T(8,128)(2,1)S(1)}, u32[]{:S(2)}, u32[]{:S(2)}) collective-permute-start(bf16[1,127,4096]{2,1,0:T(8,128)(2,1)S(1)} %slice.247), channel_id=1, source_target_pairs={{0,1},{1,2},{2,3},{3,4},{4,5},{5,6},{6,7},{7,8},{8,9},{9,10},{10,1... | collective-permute-start | bytes 3121160 | tf_op jit(solution)/shard_map/ppermute | solution.py:10
  218.8 98.4 %copy-start.7 = (bf16[1,128,4096]{2,1,0:T(8,128)(2,1)S(1)}, bf16[1,128,4096]{2,1,0:T(8,128)(2,1)}, u32[]{:S(2)}) copy-start(bf16[1,128,4096]{2,1,0:T(8,128)(2,1)} %param.15) | copy-start | bytes 3145732
  486.6 4.3 copy-start.2
  486.6 4.3 copy-start.3
  486.6 4.3 copy-start.4
  489.4 25.3 %collective-permute-start.3 = (bf16[1,6,12288]{2,1,0:T(8,128)(2,1)}, bf16[1,6,12288]{2,1,0:T(8,128)(2,1)}, u32[]{:S(2)}, u32[]{:S(2)}) collective-permute-start(bf16[1,6,12288]{2,1,0:T(8,128)(2,1)} %slice.251), channel_id=1, source_target_pairs={{1,0},{2,1},{3,2},{4,3},{5,4},{6,5},{7,6},{8,7},{9,8},{10,9},{11,1... | collective-permute-start | bytes 442376 | tf_op jit(solution)/shard_map/ppermute | solution.py:10
  512.6 5.3 copy-start.9
  512.6 5.3 copy-start.11
  512.6 5.3 copy-start.12
  512.6 5.3 copy-start.13
  512.6 5.3 copy-start.14
  512.6 5.3 copy-start.15
  512.6 5.3 copy-start.19
  512.6 5.3 copy-start.20
  512.6 5.3 copy-start.21
  512.6 5.3 copy-start.22
  512.7 5.3 copy-start.23
  512.7 5.3 copy-start.24
Sparse Core Ops, SparseCore 0:
  514.8 259.5 all-reduce.4
where the time goes:
time: 788 us; the launch traced here: 785 us
  waiting for transfers between devices  272 us (35%)
  local copies, waits for them, and re-layouts  178 us (23%)
  matrix products  174 us (22%)
  other arithmetic  89.2 us (11%)
  loops' own time  47.3 us (6%)
  between operations  14.4 us (2%)
  starting transfers between devices  10.1 us (1%)
    psum x1, waiting for transfers between devices, body(): short_total, long_total = lax.psum((short_sum, long_sum), ('dp', 'ctx'))  247 us
    dot_general x8, matrix products, one_block(): jnp.einsum('gpj,pjt->tg', products, weights, precision=lax.Precision.HIGH...  74.1 us
    dynamic_slice x32, local copies, waits for them, and re-layouts, one_block(): lax.dynamic_slice_in_dim(lax.dynamic_index_in_dim(extended, pack_index, 0...  65.5 us
    dot_general x16, matrix products, one_block(): jnp.einsum('gpj,jgc->pgc', matrix, pieces, preferred_element_type=jnp.flo...  63 us
    dynamic_update_slice x32, local copies, waits for them, and re-layouts, long_apply(): lax.map(one_block, jnp.arange(pack_count * blocks, dtype=jnp.int32))  46.3 us
    dot_general x8, matrix products, one_block(): jnp.einsum('pgc,jgc->gpj', left_parts, right_parts, preferred_element_typ...  36.5 us
    another operation x2, loops' own time, long_apply(): lax.map(one_block, jnp.arange(pack_count * blocks, dtype=jnp.int32))  31.5 us
    ppermute x4, waiting for transfers between devices, shifted_2(): return lax.ppermute(x, axis, pairs)  25.5 us
  transfers between devices with their start and end apart: 5, of which 3 were waited for; matrix products, arithmetic and copies ran while one was open for 10% of the time, Pallas kernels for 0%

commit v1 on v0

v1 whole, which is shorter than its diff:
```python
import functools

import jax
import jax.numpy as jnp
from jax import lax
from jax.experimental import pallas as pl
from jax.experimental.pallas import tpu as pltpu
from jax.sharding import PartitionSpec as P

MESH = pl.DeviceIdType.MESH
L = 128
D = 4096
TILES = D // L
W = 512
CHUNKS = D // W
U = W // L
SHORT = 7
GT = 4 * TILES
F32 = jnp.float32
BF16 = jnp.bfloat16


def kernel(nz, nctx, qkv, segs, staps, ltaps, cot, out, ig, sgo, lgo,
           hq_out, hq_in, prod, gg, short, bg, bg_out, bg_in, xs, fwd_mask, bwd_mask,
           mf, mb, mtri, seg_col, hf, hb, lane_sel, lhs_f, lhs_b, lhs_g, res_f, res_b, res_g, lag_rows,
           grads, part, half, zpart, total,
           send, recv, asend, arecv, psend, precv, zsend, zrecv, p2send, p2recv, gsend, grecv):
    dp, ctx = lax.axis_index("dp"), lax.axis_index("ctx")
    left, right = lax.rem(ctx + nctx - 1, nctx), lax.rem(ctx + 1, nctx)
    core = lax.rem(dp, 2)
    z = dp // 2
    twin = dp + 1 - 2 * core
    per = GT // nctx
    hper = per // 2

    barrier = pltpu.get_barrier_semaphore()

    def greet_ctx(k, c):
        pl.semaphore_signal(barrier, inc=1, device_id=(dp, lax.rem(ctx + k, nctx)), device_id_type=MESH)
        return c

    def greet_z(k, c):
        pl.semaphore_signal(barrier, inc=1, device_id=(lax.rem(z + k, nz) * 2 + core, ctx), device_id_type=MESH)
        return c

    lax.fori_loop(1, nctx, greet_ctx, 0)
    lax.fori_loop(1, nz, greet_z, 0)
    pl.semaphore_signal(barrier, inc=1, device_id=(twin, ctx), device_id_type=MESH)

    def pack(c, carry):
        for u in range(U):
            lane = pl.multiple_of(c * W + u * L, L)
            rows = [qkv[112:128, pl.ds(s * D + lane, L)].astype(F32)[8:16] for s in range(3)]
            hq_out[c, 0:16, u * L:(u + 1) * L] = jnp.concatenate(rows[0:2], 0).astype(BF16)
            hq_out[c, 16:32, u * L:(u + 1) * L] = jnp.concatenate([rows[2], rows[2]], 0).astype(BF16)
        return carry

    lax.fori_loop(0, CHUNKS, pack, 0)
    pl.semaphore_wait(barrier, nctx + nz - 1)

    def hq_copy(c):
        return pltpu.make_async_remote_copy(hq_out.at[c], hq_in.at[c], send.at[0, c], recv.at[0, c], device_id=(dp, right), device_id_type=MESH)

    def prod_copy(c):
        return pltpu.make_async_remote_copy(prod.at[c, pl.ds(L, L)], prod.at[c, pl.ds(0, L)], send.at[1, c], recv.at[1, c], device_id=(dp, right), device_id_type=MESH)

    def gg_copy(c):
        return pltpu.make_async_remote_copy(gg.at[c, pl.ds(0, L)], gg.at[c, pl.ds(L, L)], send.at[2, c], recv.at[2, c], device_id=(dp, left), device_id_type=MESH)

    def bg_copy(c):
        return pltpu.make_async_remote_copy(bg_out.at[c], bg_in.at[c], send.at[3, c], recv.at[3, c], device_id=(dp, left), device_id_type=MESH)

    def go(copy):
        def step(c, carry):
            copy(c).start()
            return carry
        return step

    lax.fori_loop(0, CHUNKS, go(hq_copy), 0)

    own = segs[0:1, pl.ds(pl.multiple_of(ctx * L, L), L)].astype(F32)
    prev = segs[0:1, pl.ds(pl.multiple_of(left * L, L), L)].astype(F32)
    nxt = segs[0:1, pl.ds(pl.multiple_of(right * L, L), L)].astype(F32)
    prev = jnp.where(ctx == 0, -1.0, prev)
    nxt = jnp.where(ctx == nctx - 1, -1.0, nxt)
    own_r = jnp.broadcast_to(own, (L, L))
    prev_r = jnp.broadcast_to(prev, (L, L))
    next_r = jnp.broadcast_to(nxt, (L, L))
    own_c = own_r.T
    seg_col[0:8] = prev_r.T[120:128]
    seg_col[8:136] = own_c
    seg_col[136:144] = next_r.T[0:8]
    rows = lax.broadcasted_iota(jnp.int32, (L, L), 0)
    cols = lax.broadcasted_iota(jnp.int32, (L, L), 1)
    same_own = own_c == own_r
    one = jnp.ones((L, L), F32)
    zero = jnp.zeros((L, L), F32)
    mf[:, 0:L] = jnp.where(jnp.logical_and(own_c == prev_r, rows < cols), one, zero).astype(BF16)
    mf[:, L:2 * L] = jnp.where(jnp.logical_and(same_own, rows >= cols), one, zero).astype(BF16)
    b_own = jnp.where(jnp.logical_and(same_own, cols >= rows), one, zero)
    b_next = jnp.where(jnp.logical_and(own_c == next_r, cols < rows), one, zero)
    mb[:, 0:L] = b_own.astype(BF16)
    mb[:, L:2 * L] = b_next.astype(BF16)
    mtri[0] = b_own
    mtri[1] = b_next
    for t in range(1, SHORT):
        fwd_mask[t - 1] = jnp.where(own_c == seg_col[8 - t:136 - t], one, zero)
        bwd_mask[t - 1] = jnp.where(own_c == seg_col[8 + t:136 + t], one, zero)
    eye = jnp.where(rows == cols, one, zero).astype(BF16)
    back = jnp.where(jnp.logical_or(rows + cols == L, rows + cols == 0), one, zero).astype(BF16)
    dims = (((0,), (0,)), ((), ()))
    hb[...] = lax.dot_general(ltaps[...], eye, dims, preferred_element_type=F32).reshape(TILES, 8, L)
    hf[...] = lax.dot_general(ltaps[...], back, dims, preferred_element_type=F32).reshape(TILES, 8, L)
    for g in range(8):
        lane_sel[g] = jnp.where(cols // 16 == g, one, zero).astype(BF16)

    def first(c, carry):
        hq_copy(c).wait_recv()

        def tile(u, carry):
            lane = pl.multiple_of(u * L, L)
            wide = pl.multiple_of(c * W + u * L, L)
            halo_a = hq_in[c, 0:16, pl.ds(lane, L)].astype(F32)
            halo_b = hq_in[c, 16:32, pl.ds(lane, L)].astype(F32)
            halos = (halo_a[0:8], halo_a[8:16], halo_b[0:8])
            done = []
            for s in range(3):
                at = pl.ds(s * D + wide, L)
                x = qkv[:, at].astype(F32)
                xs[s, 0:8] = halos[s]
                xs[s, 8:136] = x
                y = staps[0:1, at] * x
                for t in range(1, SHORT):
                    y = y + staps[t:t + 1, at] * (xs[s, 8 - t:136 - t] * fwd_mask[t - 1])
                y = y.astype(BF16)
                short[s, :, pl.ds(wide, L)] = y
                done.append(y.astype(F32))
            prod[c, L:2 * L, pl.ds(lane, L)] = (done[1] * done[2]).astype(BF16)
            gg[c, 0:L, pl.ds(lane, L)] = (cot[:, pl.ds(wide, L)].astype(F32) * done[0]).astype(BF16)
            return carry

        lax.fori_loop(0, U, tile, 0)
        prod_copy(c).start()
        gg_copy(c).start()
        return carry

    lax.fori_loop(0, CHUNKS, first, 0)

    lane_id = lax.broadcasted_iota(jnp.int32, (L, L), 1) // 16

    def second(c, carry):
        prod_copy(c).wait_recv()
        gg_copy(c).wait_recv()

        def tile(u, carry):
            lane = pl.multiple_of(u * L, L)
            n = c * U + u
            wide = pl.multiple_of(n * L, L)
            p_ext = prod[c, :, pl.ds(lane, L)]
            g_ext = gg[c, :, pl.ds(lane, L)]
            p_own = p_ext[L:2 * L]
            taps_f = hf[n]
            taps_b = hb[n]
            for g in range(8):
                ring = pltpu.roll(jnp.broadcast_to(taps_f[g:g + 1], (L, L)), 0, 1, stride=1, stride_axis=0).astype(BF16)
                lhs_f[g * L:(g + 1) * L, 0:L] = ring * mf[:, 0:L]
                lhs_f[g * L:(g + 1) * L, L:2 * L] = ring * mf[:, L:2 * L]
                ring = pltpu.roll(jnp.broadcast_to(taps_b[g:g + 1], (L, L)), 0, 1, stride=1, stride_axis=0).astype(BF16)
                lhs_b[g * L:(g + 1) * L, 0:L] = ring * mb[:, 0:L]
                lhs_b[g * L:(g + 1) * L, L:2 * L] = ring * mb[:, L:2 * L]
                lhs_g[g * L:(g + 1) * L] = p_own * lane_sel[g]
            res_f[...] = jnp.dot(lhs_f[...], p_ext, preferred_element_type=F32)
            res_b[...] = jnp.dot(lhs_b[...], g_ext, preferred_element_type=F32)
            res_g[...] = lax.dot_general(lhs_g[...], g_ext, (((1,), (1,)), ((), ())), preferred_element_type=F32)
            mix = res_f[0:L]
            pg = res_b[0:L]
            for g in range(1, 8):
                mix = jnp.where(lane_id == g, res_f[g * L:(g + 1) * L], mix)
                pg = jnp.where(lane_id == g, res_b[g * L:(g + 1) * L], pg)
            for g in range(8):
                acc = None
                for k in range(16):
                    r = slice(g * L + 8 * k, g * L + 8 * k + 8)
                    kk = slice(8 * k, 8 * k + 8)
                    block = res_g[r, 0:L] * mtri[0, kk] + res_g[r, L:2 * L] * mtri[1, kk]
                    if k:
                        block = pltpu.roll(block, L - 8 * k, 1)
                    acc = block if acc is None else acc + block
                lag_rows[g] = acc
            lags = lag_rows[:, 0, :]
            for k in range(1, 8):
                lags = lags + pltpu.roll(lag_rows[:, k, :], L - k, 1)
            grads[3 * TILES + n] = lags
            q = short[0, :, pl.ds(wide, L)].astype(F32)
            k = short[1, :, pl.ds(wide, L)].astype(F32)
            v = short[2, :, pl.ds(wide, L)].astype(F32)
            out[:, pl.ds(wide, L)] = (q * mix).astype(BF16)
            up = cot[:, pl.ds(wide, L)].astype(F32)
            b = [(x).astype(BF16).astype(F32) for x in (up * mix, pg * v, pg * k)]
            for s in range(3):
                bg[s * TILES + n, 0:L] = b[s]
            bg_out[c, 0:16, pl.ds(lane, L)] = jnp.concatenate([b[0][0:8], b[1][0:8]], 0).astype(BF16)
            bg_out[c, 16:32, pl.ds(lane, L)] = jnp.concatenate([b[2][0:8], b[2][0:8]], 0).astype(BF16)
            return carry

        lax.fori_loop(0, U, tile, 0)
        bg_copy(c).start()
        return carry

    def third(c, carry):
        bg_copy(c).wait_recv()

        def tile(u, carry):
            lane = pl.multiple_of(u * L, L)
            n = c * U + u
            wide = pl.multiple_of(n * L, L)
            halo_a = bg_in[c, 0:16, pl.ds(lane, L)].astype(F32)
            halo_b = bg_in[c, 16:32, pl.ds(lane, L)].astype(F32)
            halos = (halo_a[0:8], halo_a[8:16], halo_b[0:8])
            for s in range(3):
                m = s * TILES + n
                at = pl.ds(s * D + wide, L)
                bg[m, L:L + 8] = halos[s]
                x = qkv[:, at].astype(F32)
                b = bg[m, 0:L]
                y = staps[0:1, at] * b
                terms = [jnp.sum(x * b, axis=0, keepdims=True)]
                for t in range(1, SHORT):
                    b = bg[m, t:L + t] * bwd_mask[t - 1]
                    y = y + staps[t:t + 1, at] * b
                    terms.append(jnp.sum(x * b, axis=0, keepdims=True))
                ig[:, at] = y.astype(BF16)
                terms.append(jnp.zeros((1, L), F32))
                grads[m] = jnp.concatenate(terms, 0)
            return carry

        lax.fori_loop(0, U, tile, 0)
        return carry

    def both(c, carry):
        second(c, carry)

        @pl.when(c > 0)
        def _():
            third(c - 1, carry)

        return carry

    lax.fori_loop(0, CHUNKS, both, 0)
    third(CHUNKS - 1, 0)

    def scatter_copy(k):
        to = lax.rem(ctx + k, nctx)
        return pltpu.make_async_remote_copy(grads.at[pl.ds(to * per, per)], part.at[k], asend.at[k], arecv.at[k], device_id=(dp, to), device_id_type=MESH)

    lax.fori_loop(1, nctx, go(scatter_copy), 0)

    def gather_sum(k, acc):
        scatter_copy(k).wait_recv()
        return acc + part[k]

    half[0] = lax.fori_loop(1, nctx, gather_sum, grads[pl.ds(ctx * per, per)])
    pair = pltpu.make_async_remote_copy(half.at[0, pl.ds((1 - core) * hper, hper)], half.at[1, pl.ds(0, hper)], psend, precv, device_id=(twin, ctx), device_id_type=MESH)
    pair.start()
    pair.wait_recv()
    zpart[z] = half[0, pl.ds(core * hper, hper)] + half[1, 0:hper]

    def z_copy(k):
        return pltpu.make_async_remote_copy(zpart.at[z], zpart.at[z], zsend.at[k], zrecv.at[k], device_id=(lax.rem(z + k, nz) * 2 + core, ctx), device_id_type=MESH)

    def z_wait(k, carry):
        src = lax.rem(z + nz - k, nz)
        pltpu.make_async_remote_copy(zpart.at[src], zpart.at[src], zsend.at[k], zrecv.at[k], device_id=(lax.rem(z + k, nz) * 2 + core, ctx), device_id_type=MESH).wait_recv()
        return carry

    lax.fori_loop(1, nz, go(z_copy), 0)
    lax.fori_loop(1, nz, z_wait, 0)
    mine = zpart[0]
    for k in range(1, nz):
        mine = mine + zpart[k]
    base = ctx * per
    at = pl.ds(base + core * hper, hper)
    total[at] = mine
    pair2 = pltpu.make_async_remote_copy(total.at[at], total.at[at], p2send, p2recv, device_id=(twin, ctx), device_id_type=MESH)
    pair2.start()
    other = pl.ds(base + (1 - core) * hper, hper)
    pltpu.make_async_remote_copy(total.at[other], total.at[other], p2send, p2recv, device_id=(twin, ctx), device_id_type=MESH).wait_recv()

    def gather_copy(k):
        block = total.at[pl.ds(base, per)]
        return pltpu.make_async_remote_copy(block, block, gsend.at[k], grecv.at[k], device_id=(dp, lax.rem(ctx + k, nctx)), device_id_type=MESH)

    def gather_wait(k, carry):
        src = lax.rem(ctx + nctx - k, nctx)
        block = total.at[pl.ds(src * per, per)]
        pltpu.make_async_remote_copy(block, block, gsend.at[k], grecv.at[k], device_id=(dp, lax.rem(ctx + k, nctx)), device_id_type=MESH).wait_recv()
        return carry

    lax.fori_loop(1, nctx, go(gather_copy), 0)
    lax.fori_loop(1, nctx, gather_wait, 0)
    for n in range(3 * TILES):
        sgo[:, n * L:(n + 1) * L] = total[n][0:SHORT]
    lgo[...] = total[3 * TILES:].reshape(8 * TILES, L).T

    def drain(copy):
        def step(c, carry):
            copy(c).wait_send()
            return carry
        return step

    for copy in (hq_copy, prod_copy, gg_copy, bg_copy):
        lax.fori_loop(0, CHUNKS, drain(copy), 0)
    lax.fori_loop(1, nctx, drain(scatter_copy), 0)
    lax.fori_loop(1, nz, drain(z_copy), 0)
    lax.fori_loop(1, nctx, drain(gather_copy), 0)
    pair.wait_send()
    pair2.wait_send()


def body(nz, nctx, qkv, segments, short_taps, long_taps, cotangent):
    per = GT // nctx
    vmem = pl.BlockSpec(memory_space=pltpu.VMEM)
    dma = pltpu.SemaphoreType.DMA
    shape = jax.ShapeDtypeStruct
    out, ig, sg, lg = pl.pallas_call(
        functools.partial(kernel, nz, nctx),
        out_shape=(shape((L, D), BF16), shape((L, 3 * D), BF16), shape((SHORT, 3 * D), F32), shape((L, 8 * TILES), F32)),
        in_specs=[vmem] * 5,
        out_specs=[vmem] * 4,
        scratch_shapes=[
            pltpu.VMEM((CHUNKS, 32, W), BF16),
            pltpu.VMEM((CHUNKS, 32, W), BF16),
            pltpu.VMEM((CHUNKS, 2 * L, W), BF16),
            pltpu.VMEM((CHUNKS, 2 * L, W), BF16),
            pltpu.VMEM((3, L, D), BF16),
            pltpu.VMEM((3 * TILES, L + 8, L), F32),
            pltpu.VMEM((CHUNKS, 32, W), BF16),
            pltpu.VMEM((CHUNKS, 32, W), BF16),
            pltpu.VMEM((3, L + 8, L), F32),
            pltpu.VMEM((SHORT - 1, L, L), F32),
            pltpu.VMEM((SHORT - 1, L, L), F32),
            pltpu.VMEM((L, 2 * L), BF16),
            pltpu.VMEM((L, 2 * L), BF16),
            pltpu.VMEM((2, L, L), F32),
            pltpu.VMEM((L + 16, L), F32),
            pltpu.VMEM((TILES, 8, L), F32),
            pltpu.VMEM((TILES, 8, L), F32),
            pltpu.VMEM((8, L, L), BF16),
            pltpu.VMEM((8 * L, 2 * L), BF16),
            pltpu.VMEM((8 * L, 2 * L), BF16),
            pltpu.VMEM((8 * L, L), BF16),
            pltpu.VMEM((8 * L, L), F32),
            pltpu.VMEM((8 * L, L), F32),
            pltpu.VMEM((8 * L, 2 * L), F32),
            pltpu.VMEM((8, 8, L), F32),
            pltpu.VMEM((GT, 8, L), F32),
            pltpu.VMEM((nctx, per, 8, L), F32),
            pltpu.VMEM((2, per, 8, L), F32),
            pltpu.VMEM((nz, per // 2, 8, L), F32),
            pltpu.VMEM((GT, 8, L), F32),
            dma((4, CHUNKS)), dma((4, CHUNKS)),
            dma((nctx,)), dma((nctx,)),
            dma, dma,
            dma((nz,)), dma((nz,)),
            dma, dma,
            dma((nctx,)), dma((nctx,)),
        ],
        compiler_params=pltpu.CompilerParams(collective_id=0, has_side_effects=True, vmem_limit_bytes=56 * 1024 * 1024),
        cost_estimate=pl.CostEstimate(flops=20_000_000_000, bytes_accessed=10_000_000, transcendentals=0),
        name="hyena",
    )(qkv[0], segments, short_taps, long_taps, cotangent[0])
    return out[None], ig[None], sg, lg


def solution(mesh):
    in_specs = (P("dp", "ctx", None), P("dp", None), P(), P(), P("dp", "ctx", None))
    out_specs = (P("dp", "ctx", None), P("dp", "ctx", None), P(), P())
    step = functools.partial(body, mesh.shape["dp"] // 2, mesh.shape["ctx"])
    return jax.shard_map(step, mesh=mesh, in_specs=in_specs, out_specs=out_specs, check_vma=False)
```

time: 788 us -> 110 us (0.14)
  waiting for transfers between devices: 272 us -> 0 us
  matrix products: 174 us -> 0 us
  local copies, waits for them, and re-layouts: 178 us -> 7.58 us
  Pallas kernels: 0 us -> 102 us
  other arithmetic: 89.2 us -> 0 us
  loops' own time: 47.3 us -> 0 us
  between operations: 14.4 us -> 0.64 us
  starting transfers between devices: 10.1 us -> 0 us
    psum x1 -> x0, waiting for transfers between devices: 247 us -> none  [body(): short_total, long_total = lax.psum((short_sum, long_sum), ('dp', 'ctx'))]
    dot_general x32 -> x0, matrix products: 174 us -> none  [the longest x8 74.1 us: one_block(): jnp.einsum('gpj,pjt->tg', products, weights, precision=lax.Precision.HIGH...]
    pallas_call x0 -> x1, Pallas kernels: none -> 102 us  [body(): pl.pallas_call(functools.partial(kernel, nz, nctx), out_shape=(shape((L,...]
    dynamic_slice x88 -> x0, local copies, waits for them, and re-layouts: 93.8 us -> none  [the longest x32 65.5 us: one_block(): lax.dynamic_slice_in_dim(lax.dynamic_index_in_dim(extended, pack_index, 0...]
    another operation x3 -> x0, loops' own time: 47.3 us -> none  [the longest x2 31.5 us: long_apply(): lax.map(one_block, jnp.arange(pack_count * blocks, dtype=jnp.int32))]
    dynamic_update_slice x32 -> x0, local copies, waits for them, and re-layouts: 46.3 us -> none  [long_apply(): lax.map(one_block, jnp.arange(pack_count * blocks, dtype=jnp.int32))]
    ppermute x4 -> x0, waiting for transfers between devices: 25.5 us -> none  [shifted_2(): return lax.ppermute(x, axis, pairs)]
    convert_element_type x12 -> x0, other arithmetic: 23.8 us -> none  [the longest x1 9.73 us: body(): short_backward(branch_ext, seg_sbwd, short_taps).astype(jnp.bfloat16)]
  transfers between devices with their start and end apart: 5 -> 0, of which waited for: 3 -> 0; matrix products, arithmetic and copies ran while one was open for 10% -> 0% of each run, Pallas kernels for 0% -> 0%
where the time goes in v1:
time: 110 us
  Pallas kernels  102 us (93%)
  local copies, waits for them, and re-layouts  7.58 us (7%)
    pallas_call x1, Pallas kernels, body(): pl.pallas_call(functools.partial(kernel, nz, nctx), out_shape=(shape((L,...  102 us
    unnamed x8, local copies, waits for them, and re-layouts  7.58 us

profile of v1, /device:TPU:1, one launch (start us, length us, event | category | flops | bytes accessed | tf_op | source)
XLA Modules:
  0.0 109.9 jit_solution(14474922699422515171)
XLA Ops:
  0.6 101.6 %hyena.1 = (bf16[128,4096]{1,0:T(8,128)(2,1)}, bf16[128,12288]{1,0:T(8,128)(2,1)}, f32[7,12288]{1,0:T(8,128)}, f32[128,256]{1,0:T(8,128)}) custom-call(bf16[128,12288]{1,0:T(8,128)(2,1)} %bitcast.6, s32[1,2048]{1,0:T(1,128)} %segs.1, f32[7,12288]{1,0:T(8,128)} %staps.1, bf16[128,256]{1,0:T(8,128)(2,1)} %ltaps.1, bf16[128,4096]{1,0:T(8,128)(2,1)} %bitcast.7), custom_call_target="tpu_custom_call" | custom-call | flops 20000000000 | bytes 10000000 | tf_op jit(solution)/shard_map/hyena/pallas_call | solution.py:325
  102.3 2.3 %copy.13 = bf16[1,128,4096]{2,1,0:T(8,128)(2,1)} copy(bf16[1,128,4096]{2,1,0:T(8,128)(2,1)} %bitcast.5) | data formatting | bytes 2097152
  104.6 0.0 copy-start
  104.6 0.0 copy-start.1
  104.6 3.9 %copy.14 = bf16[1,128,12288]{2,1,0:T(8,128)(2,1)} copy(bf16[1,128,12288]{2,1,0:T(8,128)(2,1)} %bitcast.4) | data formatting | bytes 6291456
  108.5 0.0 copy-done
  108.5 0.7 copy.15
  109.2 0.0 copy-done.1
  109.2 0.7 copy.16
Async XLA Ops:
  104.6 3.9 %copy-start = (f32[7,12288]{1,0:T(8,128)S(1)}, f32[7,12288]{1,0:T(8,128)}, u32[]{:S(2)}) copy-start(f32[7,12288]{1,0:T(8,128)} %get-tuple-element.18) | copy-start | bytes 1032196
  104.6 4.6 %copy-start.1 = (f32[128,256]{1,0:T(8,128)S(1)}, f32[128,256]{1,0:T(8,128)}, u32[]{:S(2)}) copy-start(f32[128,256]{1,0:T(8,128)} %get-tuple-element.19) | copy-start | bytes 393220

commit v2 on v1

v2 whole, which is shorter than its diff:
```python
import functools

import jax
import jax.numpy as jnp
from jax import lax
from jax.experimental import pallas as pl
from jax.experimental.pallas import tpu as pltpu
from jax.sharding import PartitionSpec as P

MESH = pl.DeviceIdType.MESH
L = 128
D = 4096
TILES = D // L
W = 256
CHUNKS = D // W
U = W // L
SHORT = 7
H = 16
SIDE = 4
SUPER = CHUNKS // 2
SPANS = ((0, 4), (4, 4))
LOOP_STAGES = ((11, "a", 0), (12, "b", 0), (14, "c", 0), (15, "d", 0))
PART = 4
EARLY = 8
AHEAD = 3
ROWS = 16
LAG = 4
F32 = jnp.float32
BF16 = jnp.bfloat16


def kernel(nz, qkv_hbm, segs_hbm, staps_hbm, ltaps_hbm, cot_hbm, out_hbm, ig_hbm, sgo, lgo,
           qkv, segs, staps, ltaps, cot, out, ig, hq_out, hq_in, prod, gg, short, bg, bg_out, bg_in, xs, xh, fwd_mask, bwd_mask,
           mf, mb, mtri, seg_col, hf, hb, lane_sel, lag_rows, lag_all,
           grads, twin_in, z_in, y_in, x_in, total,
           load, store, hsend, hrecv, psend, precv, csend, crecv, bsend, brecv, tsend, trecv, rsend, rrecv, ysend, yrecv, xsend, xrecv, gsend, grecv):
    nctx, ndp = SIDE * SIDE, 2 * nz
    dp, ctx = lax.axis_index("dp"), lax.axis_index("ctx")
    core, z = lax.rem(dp, 2), dp // 2
    left, right = lax.rem(ctx + nctx - 1, nctx), lax.rem(ctx + 1, nctx)
    my_x, my_y = ctx // SIDE, lax.rem(ctx, SIDE)
    y_at = [my_x * SIDE + lax.rem(my_y + k, SIDE) for k in range(SIDE)]
    x_at = [lax.rem(my_x + k, SIDE) * SIDE + my_y for k in range(SIDE)]

    loads = [pltpu.make_async_copy(src, dst, load.at[i]) for i, (src, dst) in enumerate(
        ((segs_hbm, segs), (ltaps_hbm, ltaps), (staps_hbm, staps), (qkv_hbm, qkv), (cot_hbm, cot)))]
    for one_load in loads:
        one_load.start()

    barrier = pltpu.get_barrier_semaphore()

    def greet_dp(k, c):
        pl.semaphore_signal(barrier, inc=1, device_id=(lax.rem(dp + k, ndp), ctx), device_id_type=MESH)
        return c

    lax.fori_loop(1, ndp, greet_dp, 0)
    for to in [left, right] + y_at[1:] + x_at[1:]:
        pl.semaphore_signal(barrier, inc=1, device_id=(dp, to), device_id_type=MESH)

    def hop(src, dst, s, r, to):
        return pltpu.make_async_remote_copy(src, dst, s, r, device_id=(dp, to), device_id_type=MESH)

    def part(i):
        return pl.ds(i * PART, PART)

    def hq_copy(i):
        return hop(hq_out.at[part(i)], hq_in.at[part(i)], hsend.at[0, i], hrecv.at[0, i], right)

    def prod_head(i):
        return hop(prod.at[part(i), pl.ds(L, H)], prod.at[part(i), pl.ds(0, H)], hsend.at[1, i], hrecv.at[1, i], right)

    def gg_head(i):
        return hop(gg.at[part(i), pl.ds(0, H)], gg.at[part(i), pl.ds(L, H)], hsend.at[2, i], hrecv.at[2, i], left)

    def prod_copy(c):
        return hop(prod.at[c, pl.ds(L + H, L - H)], prod.at[c, pl.ds(H, L - H)], psend.at[c], precv.at[c], right)

    def gg_copy(c):
        return hop(gg.at[c, pl.ds(H, L - H)], gg.at[c, pl.ds(L + H, L - H)], csend.at[c], crecv.at[c], left)

    def bg_copy(c):
        return hop(bg_out.at[c], bg_in.at[c], bsend.at[c], brecv.at[c], left)

    def out_copy(c):
        at = pl.ds(pl.multiple_of(c * W, W), W)
        return pltpu.make_async_copy(out.at[:, at], out_hbm.at[:, at], store.at[0, c])

    def ig_copy(c, s):
        at = pl.ds(pl.multiple_of(s * D + c * W, W), W)
        return pltpu.make_async_copy(ig.at[:, at], ig_hbm.at[:, at], store.at[1 + s, c])

    loads[0].wait()
    own = segs[0:1, pl.ds(pl.multiple_of(ctx * L, L), L)].astype(F32)
    prev = segs[0:1, pl.ds(pl.multiple_of(left * L, L), L)].astype(F32)
    nxt = segs[0:1, pl.ds(pl.multiple_of(right * L, L), L)].astype(F32)
    prev = jnp.where(ctx == 0, -1.0, prev)
    nxt = jnp.where(ctx == nctx - 1, -1.0, nxt)
    own_r = jnp.broadcast_to(own, (L, L))
    prev_r = jnp.broadcast_to(prev, (L, L))
    next_r = jnp.broadcast_to(nxt, (L, L))
    own_c = own_r.T
    seg_col[0:8] = prev_r.T[120:128]
    seg_col[8:136] = own_c
    seg_col[136:144] = next_r.T[0:8]
    rows = lax.broadcasted_iota(jnp.int32, (L, L), 0)
    cols = lax.broadcasted_iota(jnp.int32, (L, L), 1)
    same_own = own_c == own_r
    one = jnp.ones((L, L), F32)
    zero = jnp.zeros((L, L), F32)
    mf[:, 0:L] = jnp.where(jnp.logical_and(own_c == prev_r, rows < cols), one, zero).astype(BF16)
    mf[:, L:2 * L] = jnp.where(jnp.logical_and(same_own, rows >= cols), one, zero).astype(BF16)
    b_own = jnp.where(jnp.logical_and(same_own, cols >= rows), one, zero)
    b_next = jnp.where(jnp.logical_and(own_c == next_r, cols < rows), one, zero)
    mb[:, 0:L] = b_own.astype(BF16)
    mb[:, L:2 * L] = b_next.astype(BF16)
    mtri[0] = b_own
    mtri[1] = b_next
    for t in range(1, SHORT):
        fwd_mask[t - 1] = jnp.where(own_c == seg_col[8 - t:136 - t], one, zero)
        bwd_mask[t - 1] = jnp.where(own_c == seg_col[8 + t:136 + t], one, zero)
    loads[1].wait()
    eye = jnp.where(rows == cols, one, zero).astype(BF16)
    back = jnp.where(jnp.logical_or(rows + cols == L, rows + cols == 0), one, zero).astype(BF16)
    dims = (((0,), (0,)), ((), ()))
    hb[...] = lax.dot_general(ltaps[...], eye, dims, preferred_element_type=F32).reshape(TILES, 8, L)
    hf[...] = lax.dot_general(ltaps[...], back, dims, preferred_element_type=F32).reshape(TILES, 8, L)
    for g in range(8):
        lane_sel[g] = jnp.where(cols // 16 == g, one, zero).astype(BF16)
    lane_id = cols // 16

    for one_load in loads[2:]:
        one_load.wait()

    def pack(dst, c, parts):
        flat = [parts[u][s] for u in range(U) for s in range(3)]
        for k in range(0, 3 * U, 2):
            dst[c, 8 * k:8 * k + 16] = jnp.concatenate(flat[k:k + 2], 0).astype(BF16)

    def unpack(src, c):
        flat = []
        for k in range(0, 3 * U, 2):
            two = src[c, 8 * k:8 * k + 16].astype(F32)
            flat += [two[0:8], two[8:16]]
        return [flat[3 * u:3 * u + 3] for u in range(U)]

    def lanes(c, u):
        return pl.multiple_of(c * W + u * L, L)

    def pack_last(c, carry):
        pack(hq_out, c, [[qkv[L - 16:L, pl.ds(s * D + lanes(c, u), L)].astype(F32)[8:16] for s in range(3)] for u in range(U)])
        return carry

    lax.fori_loop(0, CHUNKS, pack_last, 0)

    def gates(c, u, r0, r1, done):
        here = slice(u * L, (u + 1) * L)
        wide = pl.ds(lanes(c, u), L)
        y = [d.astype(BF16) for d in done]
        for s in range(3):
            short[s, r0:r1, wide] = y[s]
        q, k, v = [d.astype(F32) for d in y]
        prod[c, L + r0:L + r1, here] = (k * v).astype(BF16)
        gg[c, r0:r1, here] = (cot[r0:r1, wide].astype(F32) * q).astype(BF16)

    def first(c, carry):
        for u in range(U):
            done = []
            for s in range(3):
                at = pl.ds(s * D + lanes(c, u), L)
                k = u * 3 + s
                x = qkv[:, at].astype(F32)
                xs[k] = x
                y = staps[0:1, at] * x[H:L]
                for t in range(1, SHORT):
                    y = y + staps[t:t + 1, at] * (xs[k, H - t:L - t] * fwd_mask[t - 1, H:L])
                done.append(y)
            gates(c, u, H, L, done)
        return carry

    lax.fori_loop(0, EARLY, first, 0)
    pl.semaphore_wait(barrier, ndp - 1 + 2 + 2 * (SIDE - 1))
    for i in range(CHUNKS // PART):
        hq_copy(i).start()
    for c in range(AHEAD):
        gg_copy(c).start()
    lax.fori_loop(EARLY, CHUNKS, first, 0)
    for c in range(AHEAD):
        prod_copy(c).start()

    def first_rows(c, carry):
        halos = unpack(hq_in, c)
        for u in range(U):
            done = []
            for s in range(3):
                at = pl.ds(s * D + lanes(c, u), L)
                k = u * 3 + s
                x = qkv[0:H, at].astype(F32)
                xh[k, 0:8] = halos[u][s]
                xh[k, 8:8 + H] = x
                y = staps[0:1, at] * x
                for t in range(1, SHORT):
                    y = y + staps[t:t + 1, at] * (xh[k, 8 - t:8 + H - t] * fwd_mask[t - 1, 0:H])
                done.append(y)
            gates(c, u, 0, H, done)
        return carry

    def first_part(i, carry):
        hq_copy(i).wait_recv()
        lax.fori_loop(i * PART, (i + 1) * PART, first_rows, 0)
        prod_head(i).start()
        gg_head(i).start()
        return carry

    lax.fori_loop(0, CHUNKS // PART, first_part, 0)

    def second(c):
        parts = []
        for u in range(U):
            here = slice(u * L, (u + 1) * L)
            n = c * U + u
            wide = pl.ds(lanes(c, u), L)
            p_ext = prod[c, :, here]
            g_ext = gg[c, :, here]
            p_own = p_ext[L:2 * L]
            taps_f = hf[n]
            taps_b = hb[n]
            mix = pg = None
            for g in range(8):
                rf = pltpu.roll(jnp.broadcast_to(taps_f[g:g + 1], (L, L)), 0, 1, stride=1, stride_axis=0).astype(BF16)
                rb = pltpu.roll(jnp.broadcast_to(taps_b[g:g + 1], (L, L)), 0, 1, stride=1, stride_axis=0).astype(BF16)
                lf = jnp.concatenate([rf * mf[:, 0:L], rf * mf[:, L:2 * L]], 1)
                lb = jnp.concatenate([rb * mb[:, 0:L], rb * mb[:, L:2 * L]], 1)
                r1 = jnp.dot(lf, p_ext, preferred_element_type=F32)
                r2 = jnp.dot(lb, g_ext, preferred_element_type=F32)
                rg = lax.dot_general(p_own * lane_sel[g], g_ext, (((1,), (1,)), ((), ())), preferred_element_type=F32)
                mix = r1 if mix is None else jnp.where(lane_id == g, r1, mix)
                pg = r2 if pg is None else jnp.where(lane_id == g, r2, pg)
                acc = None
                for k in range(16):
                    r = slice(8 * k, 8 * k + 8)
                    block = rg[r, 0:L] * mtri[0, r] + rg[r, L:2 * L] * mtri[1, r]
                    if k:
                        block = pltpu.roll(block, L - 8 * k, 1)
                    acc = block if acc is None else acc + block
                lag_rows[u, g] = acc
            lags = lag_rows[u, :, 0, :]
            for k in range(1, 8):
                lags = lags + pltpu.roll(lag_rows[u, :, k, :], L - k, 1)
            grads[12 + lax.rem(c, 2) * U + u, c // 2] = lags
            q = short[0, :, wide].astype(F32)
            k = short[1, :, wide].astype(F32)
            v = short[2, :, wide].astype(F32)
            out[:, wide] = (q * mix).astype(BF16)
            up = cot[:, wide].astype(F32)
            b = [x.astype(BF16).astype(F32) for x in (up * mix, pg * v, pg * k)]
            for s in range(3):
                bg[c, u * 3 + s, 0:L] = b[s]
            parts.append([x[0:8] for x in b])
        pack(bg_out, c, parts)

    def third(c):
        halos = unpack(bg_in, c)
        for u in range(U):
            for s in range(3):
                bg[c, u * 3 + s, L:L + 8] = halos[u][s]
        return [functools.partial(third_stream, c, s) for s in range(3)]

    def third_stream(c, s):
        ats = [pl.ds(s * D + lanes(c, u), L) for u in range(U)]
        sums = [[None] * SHORT for _ in range(U)]
        for r in range(0, L, ROWS):
            marks = [bwd_mask[t - 1, r:r + ROWS] for t in range(1, SHORT)]
            for u in range(U):
                m = u * 3 + s
                x = qkv[r:r + ROWS, ats[u]].astype(F32)
                y = None
                for t in range(SHORT):
                    b = bg[c, m, r + t:r + t + ROWS]
                    if t:
                        b = b * marks[t - 1]
                    w = staps[t:t + 1, ats[u]] * b
                    y = w if y is None else y + w
                    p = x * b
                    p = functools.reduce(jnp.add, [p[k:k + 8] for k in range(0, ROWS, 8)])
                    sums[u][t] = p if sums[u][t] is None else sums[u][t] + p
                ig[r:r + ROWS, ats[u]] = y.astype(BF16)
        for u in range(U):
            terms = [jnp.sum(p, axis=0, keepdims=True) for p in sums[u]] + [jnp.zeros((1, L), F32)]
            grads[s * 4 + lax.rem(c, 2) * U + u, c // 2] = jnp.concatenate(terms, 0)

    def span(b):
        return pl.ds(*SPANS[b])

    def pairs(b):
        return pl.ds(SPANS[b][0] // 2, SPANS[b][1] // 2)

    def along(src, dst, s, r, k):
        return pltpu.make_async_remote_copy(src, dst, s, r, device_id=(lax.rem(dp + k, ndp), ctx), device_id_type=MESH)

    twin = dp + 1 - 2 * core
    mine = core * nz

    def twin_copy(b):
        src = grads.at[pl.ds(nz - mine, nz), span(b)]
        return pltpu.make_async_remote_copy(src, twin_in.at[:, span(b)], tsend.at[b], trecv.at[b], device_id=(twin, ctx), device_id_type=MESH)

    def z_copy(b, k, owner):
        return pltpu.make_async_remote_copy(grads.at[mine + owner, span(b)], z_in.at[k, span(b)], rsend.at[b, k], rrecv.at[b, k],
                                            device_id=(2 * lax.rem(z + k, nz) + core, ctx), device_id_type=MESH)

    def ag_all(b):
        block = total.at[pl.ds(1, ndp - 1), pairs(b)]
        return along(block, block, gsend.at[b], grecv.at[b], 1)

    def y_copy(b, k, slot):
        return hop(y_in.at[slot, span(b)], y_in.at[slot, span(b)], ysend.at[b, k], yrecv.at[b, k], y_at[k])

    def x_copy(b, k, slot):
        return hop(x_in.at[slot, span(b)], x_in.at[slot, span(b)], xsend.at[b, k], xrecv.at[b, k], x_at[k])

    def stage_a(b):
        twin_copy(b).start()

    def stage_b(b):
        twin_copy(b).wait_recv()
        both = grads[pl.ds(mine, nz), span(b)] + twin_in[:, span(b)]
        grads[pl.ds(mine, nz), span(b)] = both
        for k in range(1, nz):
            z_copy(b, k, lax.rem(z + k, nz)).start()

    def stage_c(b):
        acc = grads[mine + z, span(b)]
        for k in range(1, nz):
            z_copy(b, k, z).wait_recv()
            acc = acc + z_in[k, span(b)]
        y_in[my_y, span(b)] = acc
        for k in range(1, SIDE):
            y_copy(b, k, my_y).start()

    def stage_d(b):
        for k in range(1, SIDE):
            y_copy(b, k, lax.rem(my_y + SIDE - k, SIDE)).wait_recv()
        x_in[my_x, span(b)] = (y_in[0, span(b)] + y_in[1, span(b)]) + (y_in[2, span(b)] + y_in[3, span(b)])
        for k in range(1, SIDE):
            x_copy(b, k, my_x).start()

    def stage_e(b):
        for k in range(1, SIDE):
            x_copy(b, k, lax.rem(my_x + SIDE - k, SIDE)).wait_recv()
        summed = (x_in[0, span(b)] + x_in[1, span(b)]) + (x_in[2, span(b)] + x_in[3, span(b)])
        total[mine + z, pairs(b)] = summed.reshape(SPANS[b][1] // 2, 16, L).astype(BF16)

        def step(k, carry):
            block = total.at[mine + z, pairs(b)]
            along(block, block, gsend.at[b], grecv.at[b], k).start()
            return carry
        lax.fori_loop(1, ndp, step, 0)

    def take(c):
        @pl.when(lax.rem(c, PART) == 0)
        def _():
            prod_head(c // PART).wait_recv()
            gg_head(c // PART).wait_recv()

        prod_copy(c).wait_recv()
        gg_copy(c).wait_recv()

        @pl.when(c + AHEAD < CHUNKS)
        def _():
            prod_copy(c + AHEAD).start()
            gg_copy(c + AHEAD).start()

    def give(c):
        bg_copy(c).start()
        out_copy(c).start()

    def keep(c):
        for s in range(3):
            ig_copy(c, s).start()

    def ramp(c, carry):
        take(c)
        second(c)
        give(c)
        return carry

    def steady(c, carry):
        take(c)
        bg_copy(c - LAG).wait_recv()
        second(c)
        for unit in third(c - LAG):
            unit()
        give(c)
        keep(c - LAG)
        for when, stage, b in LOOP_STAGES:
            pl.when(c == when)(functools.partial(stages[stage], b))
        return carry

    stages = {"a": stage_a, "b": stage_b, "c": stage_c, "d": stage_d, "e": stage_e}
    lax.fori_loop(0, LAG, ramp, 0)
    lax.fori_loop(LAG, CHUNKS, steady, 0)

    def rest(c, carry):
        bg_copy(c).wait_recv()
        for unit in third(c):
            unit()
        keep(c)
        return carry

    stage_e(0)
    lax.fori_loop(CHUNKS - LAG, CHUNKS, rest, 0)
    for stage in stages.values():
        stage(1)
    for b in range(len(SPANS)):
        ag_all(b).wait_recv()
    for j in range(16):
        for pair in range(SUPER // 2):
            two = total[j, pair].astype(F32)
            for k in range(2):
                n = 4 * (2 * pair + k) + j % 4
                block = two[8 * k:8 * k + 8]
                if j < 12:
                    at = (j // 4) * D + n * L
                    sgo[:, at:at + L] = block[0:SHORT]
                else:
                    lag_all[8 * n:8 * n + 8] = block
    lgo[...] = lag_all[...].T

    for i in range(CHUNKS // PART):
        hq_copy(i).wait_send()
        prod_head(i).wait_send()
        gg_head(i).wait_send()

    def drain(c, carry):
        prod_copy(c).wait_send()
        gg_copy(c).wait_send()
        bg_copy(c).wait_send()
        out_copy(c).wait()
        for s in range(3):
            ig_copy(c, s).wait()
        return carry

    lax.fori_loop(0, CHUNKS, drain, 0)

    for b in range(len(SPANS)):
        twin_copy(b).wait_send()
        for k in range(1, nz):
            z_copy(b, k, lax.rem(z + k, nz)).wait_send()
        ag_all(b).wait_send()
        for k in range(1, SIDE):
            y_copy(b, k, my_y).wait_send()
            x_copy(b, k, my_x).wait_send()


def place(*refs):
    for i in range(4):
        refs[4 + i][...] = refs[i][...]


def body(nz, qkv, segments, short_taps, long_taps, cotangent):
    ndp = 2 * nz
    vmem = pl.BlockSpec(memory_space=pltpu.VMEM)
    anywhere = pl.BlockSpec(memory_space=pl.ANY)
    dma = pltpu.SemaphoreType.DMA
    shape = jax.ShapeDtypeStruct
    outs = (shape((L, D), BF16), shape((L, 3 * D), BF16), shape((SHORT, 3 * D), F32), shape((L, 8 * TILES), F32))
    results = pl.pallas_call(
        functools.partial(kernel, nz),
        out_shape=outs,
        in_specs=[pl.BlockSpec(memory_space=pltpu.HBM)] * 5,
        out_specs=[anywhere, anywhere, vmem, vmem],
        scratch_shapes=[
            pltpu.VMEM((L, 3 * D), BF16),
            pltpu.VMEM((1, 16 * L), jnp.int32),
            pltpu.VMEM((SHORT, 3 * D), F32),
            pltpu.VMEM((L, 8 * TILES), BF16),
            pltpu.VMEM((L, D), BF16),
            pltpu.VMEM((L, D), BF16),
            pltpu.VMEM((L, 3 * D), BF16),
            pltpu.VMEM((CHUNKS, 24 * U, L), BF16),
            pltpu.VMEM((CHUNKS, 24 * U, L), BF16),
            pltpu.VMEM((CHUNKS, 2 * L, W), BF16),
            pltpu.VMEM((CHUNKS, 2 * L, W), BF16),
            pltpu.VMEM((3, L, D), BF16),
            pltpu.VMEM((CHUNKS, 3 * U, L + 8, L), F32),
            pltpu.VMEM((CHUNKS, 24 * U, L), BF16),
            pltpu.VMEM((CHUNKS, 24 * U, L), BF16),
            pltpu.VMEM((3 * U, L, L), F32),
            pltpu.VMEM((3 * U, 8 + H, L), F32),
            pltpu.VMEM((SHORT - 1, L, L), F32),
            pltpu.VMEM((SHORT - 1, L, L), F32),
            pltpu.VMEM((L, 2 * L), BF16),
            pltpu.VMEM((L, 2 * L), BF16),
            pltpu.VMEM((2, L, L), F32),
            pltpu.VMEM((L + 16, L), F32),
            pltpu.VMEM((TILES, 8, L), F32),
            pltpu.VMEM((TILES, 8, L), F32),
            pltpu.VMEM((8, L, L), BF16),
            pltpu.VMEM((U, 8, 8, L), F32),
            pltpu.VMEM((8 * TILES, L), F32),
            pltpu.VMEM((ndp, SUPER, 8, L), F32),
            pltpu.VMEM((nz, SUPER, 8, L), F32),
            pltpu.VMEM((nz, SUPER, 8, L), F32),
            pltpu.VMEM((SIDE, SUPER, 8, L), F32),
            pltpu.VMEM((SIDE, SUPER, 8, L), F32),
            pltpu.VMEM((ndp, SUPER // 2, 16, L), BF16),
            dma((5,)), dma((4, CHUNKS)),
            dma((3, CHUNKS // PART)), dma((3, CHUNKS // PART)),
            dma((CHUNKS,)), dma((CHUNKS,)), dma((CHUNKS,)), dma((CHUNKS,)), dma((CHUNKS,)), dma((CHUNKS,)),
            dma((len(SPANS),)), dma((len(SPANS),)),
            dma((len(SPANS), nz)), dma((len(SPANS), nz)),
            dma((len(SPANS), SIDE)), dma((len(SPANS), SIDE)), dma((len(SPANS), SIDE)), dma((len(SPANS), SIDE)),
            dma((len(SPANS),)), dma((len(SPANS),)),
        ],
        compiler_params=pltpu.CompilerParams(collective_id=0, has_side_effects=True, vmem_limit_bytes=62 * 1024 * 1024),
        cost_estimate=pl.CostEstimate(flops=20_000_000_000, bytes_accessed=10_000_000, transcendentals=0),
        name="hyena",
    )(qkv[0], segments, short_taps, long_taps, cotangent[0])
    steps = 8
    specs = [pl.BlockSpec((L // steps, D), lambda i: (i, 0)), pl.BlockSpec((L // steps, 3 * D), lambda i: (i, 0)),
             pl.BlockSpec((SHORT, 3 * D // steps), lambda i: (0, i)), pl.BlockSpec((L // steps, 8 * TILES), lambda i: (i, 0))]
    out, ig, sg, lg = pl.pallas_call(
        place,
        grid=(steps,),
        out_shape=outs,
        in_specs=specs,
        out_specs=specs,
        name="place",
    )(*results)
    return out[None], ig[None], sg, lg


def solution(mesh):
    in_specs = (P("dp", "ctx", None), P("dp", None), P(), P(), P("dp", "ctx", None))
    out_specs = (P("dp", "ctx", None), P("dp", "ctx", None), P(), P())
    step = functools.partial(body, mesh.shape["dp"] // 2)
    return jax.shard_map(step, mesh=mesh, in_specs=in_specs, out_specs=out_specs, check_vma=False)
```

time: 110 us -> 95 us (0.86)
  Pallas kernels: 102 us -> 94.1 us
  local copies, waits for them, and re-layouts: 7.58 us -> 0 us
    unnamed x8 -> x0, local copies, waits for them, and re-layouts: 7.58 us -> none
    pallas_call x1 -> x2, Pallas kernels: 102 us -> 94.1 us  [the longest x1 87.5 us: body(): pl.pallas_call(functools.partial(kernel, nz), out_shape=outs, in_specs=[p...]
where the time goes in v2:
time: 95 us; the launch traced here: 94.8 us
  Pallas kernels  94.1 us (99%)
    pallas_call x1, Pallas kernels, body(): pl.pallas_call(functools.partial(kernel, nz), out_shape=outs, in_specs=[p...  87.5 us
    pallas_call x1, Pallas kernels, body(): pl.pallas_call(place, grid=(steps,), out_shape=outs, in_specs=specs, out_...  6.65 us

profile of v2, /device:TPU:1, one launch (start us, length us, event | category | flops | bytes accessed | tf_op | source)
XLA Modules:
  0.0 94.8 jit_solution(14780324438817635627)
XLA Ops:
  0.6 87.5 %hyena.1 = (bf16[128,4096]{1,0:T(8,128)(2,1)}, bf16[128,12288]{1,0:T(8,128)(2,1)}, f32[7,12288]{1,0:T(8,128)}, f32[128,256]{1,0:T(8,128)}) custom-call(bf16[128,12288]{1,0:T(8,128)(2,1)} %bitcast.4, s32[1,2048]{1,0:T(1,128)} %segs_hbm.1, f32[7,12288]{1,0:T(8,128)} %staps_hbm.1, bf16[128,256]{1,0:T(8,128)(2,1)} %ltaps_hbm.1, bf16[128,4096]{1,0:T(8,128)(2,1)} %bitcast.6), custom_call_target="tpu_custom_call" | custom-call | flops 20000000000 | bytes 10000000 | tf_op jit(solution)/shard_map/hyena/pallas_call | solution.py:467
  88.1 6.6 %place.1 = (bf16[128,4096]{1,0:T(8,128)(2,1)}, bf16[128,12288]{1,0:T(8,128)(2,1)}, f32[7,12288]{1,0:T(8,128)}, f32[128,256]{1,0:T(8,128)}) custom-call(bf16[128,4096]{1,0:T(8,128)(2,1)} %get-tuple-element.12.refs_0_, bf16[128,12288]{1,0:T(8,128)(2,1)} %get-tuple-element.13.refs_1_, f32[7,12288]{1,0:T(8,128)} %get-tuple-element.14.refs_2_, ...), custom_call_target="tpu_custom_call" | custom-call | tf_op jit(solution)/shard_map/place/pallas_call | solution.py:522

commit v3 on v2

--- a/solution.py
+++ b/solution.py
@@ -19,7 +19,8 @@
 SIDE = 4
 SUPER = CHUNKS // 2
 SPANS = ((0, 4), (4, 4))
-LOOP_STAGES = ((11, "a", 0), (12, "b", 0), (14, "c", 0), (15, "d", 0))
+LOOP_STAGES = ((11, "a", 0), (14, "b", 0))
+STEPS = 4
 PART = 4
 EARLY = 8
 AHEAD = 3
@@ -291,9 +292,6 @@
     def span(b):
         return pl.ds(*SPANS[b])
 
-    def pairs(b):
-        return pl.ds(SPANS[b][0] // 2, SPANS[b][1] // 2)
-
     def along(src, dst, s, r, k):
         return pltpu.make_async_remote_copy(src, dst, s, r, device_id=(lax.rem(dp + k, ndp), ctx), device_id_type=MESH)
 
@@ -308,15 +306,18 @@
         return pltpu.make_async_remote_copy(grads.at[mine + owner, span(b)], z_in.at[k, span(b)], rsend.at[b, k], rrecv.at[b, k],
                                             device_id=(2 * lax.rem(z + k, nz) + core, ctx), device_id_type=MESH)
 
-    def ag_all(b):
-        block = total.at[pl.ds(1, ndp - 1), pairs(b)]
-        return along(block, block, gsend.at[b], grecv.at[b], 1)
-
-    def y_copy(b, k, slot):
-        return hop(y_in.at[slot, span(b)], y_in.at[slot, span(b)], ysend.at[b, k], yrecv.at[b, k], y_at[k])
-
-    def x_copy(b, k, slot):
-        return hop(x_in.at[slot, span(b)], x_in.at[slot, span(b)], xsend.at[b, k], xrecv.at[b, k], x_at[k])
+    def total_copy(k):
+        return along(total.at[mine + z], total.at[mine + z], gsend, grecv, k)
+
+    def total_all():
+        block = total.at[pl.ds(1, ndp - 1)]
+        return along(block, block, gsend, grecv, 1)
+
+    def y_copy(k, slot):
+        return hop(y_in.at[slot], y_in.at[slot], ysend.at[k], yrecv.at[k], y_at[k])
+
+    def x_copy(k, slot):
+        return hop(x_in.at[slot], x_in.at[slot], xsend.at[k], xrecv.at[k], x_at[k])
 
     def stage_a(b):
         twin_copy(b).start()
@@ -328,31 +329,31 @@
         for k in range(1, nz):
             z_copy(b, k, lax.rem(z + k, nz)).start()
 
-    def stage_c(b):
-        acc = grads[mine + z, span(b)]
-        for k in range(1, nz):
-            z_copy(b, k, z).wait_recv()
-            acc = acc + z_in[k, span(b)]
-        y_in[my_y, span(b)] = acc
+    def stage_c():
+        for b in range(len(SPANS)):
+            acc = grads[mine + z, span(b)]
+            for k in range(1, nz):
+                z_copy(b, k, z).wait_recv()
+                acc = acc + z_in[k, span(b)]
+            y_in[my_y, span(b)] = acc
         for k in range(1, SIDE):
-            y_copy(b, k, my_y).start()
-
-    def stage_d(b):
+            y_copy(k, my_y).start()
+
+    def stage_d():
         for k in range(1, SIDE):
-            y_copy(b, k, lax.rem(my_y + SIDE - k, SIDE)).wait_recv()
-        x_in[my_x, span(b)] = (y_in[0, span(b)] + y_in[1, span(b)]) + (y_in[2, span(b)] + y_in[3, span(b)])
+            y_copy(k, lax.rem(my_y + SIDE - k, SIDE)).wait_recv()
+        x_in[my_x] = (y_in[0] + y_in[1]) + (y_in[2] + y_in[3])
         for k in range(1, SIDE):
-            x_copy(b, k, my_x).start()
-
-    def stage_e(b):
+            x_copy(k, my_x).start()
+
+    def stage_e():
         for k in range(1, SIDE):
-            x_copy(b, k, lax.rem(my_x + SIDE - k, SIDE)).wait_recv()
-        summed = (x_in[0, span(b)] + x_in[1, span(b)]) + (x_in[2, span(b)] + x_in[3, span(b)])
-        total[mine + z, pairs(b)] = summed.reshape(SPANS[b][1] // 2, 16, L).astype(BF16)
+            x_copy(k, lax.rem(my_x + SIDE - k, SIDE)).wait_recv()
+        summed = (x_in[0] + x_in[1]) + (x_in[2] + x_in[3])
+        total[mine + z] = summed.reshape(SUPER // 2, 16, L).astype(BF16)
 
         def step(k, carry):
-            block = total.at[mine + z, pairs(b)]
-            along(block, block, gsend.at[b], grecv.at[b], k).start()
+            total_copy(k).start()
             return carry
         lax.fori_loop(1, ndp, step, 0)
 
@@ -396,7 +397,7 @@
             pl.when(c == when)(functools.partial(stages[stage], b))
         return carry
 
-    stages = {"a": stage_a, "b": stage_b, "c": stage_c, "d": stage_d, "e": stage_e}
+    stages = {"a": stage_a, "b": stage_b}
     lax.fori_loop(0, LAG, ramp, 0)
     lax.fori_loop(LAG, CHUNKS, steady, 0)
 
@@ -407,12 +408,13 @@
         keep(c)
         return carry
 
-    stage_e(0)
     lax.fori_loop(CHUNKS - LAG, CHUNKS, rest, 0)
-    for stage in stages.values():
-        stage(1)
-    for b in range(len(SPANS)):
-        ag_all(b).wait_recv()
+    stage_a(1)
+    stage_b(1)
+    stage_c()
+    stage_d()
+    stage_e()
+    total_all().wait_recv()
     for j in range(16):
         for pair in range(SUPER // 2):
             two = total[j, pair].astype(F32)
@@ -446,15 +448,28 @@
         twin_copy(b).wait_send()
         for k in range(1, nz):
             z_copy(b, k, lax.rem(z + k, nz)).wait_send()
-        ag_all(b).wait_send()
-        for k in range(1, SIDE):
-            y_copy(b, k, my_y).wait_send()
-            x_copy(b, k, my_x).wait_send()
-
-
-def place(*refs):
-    for i in range(4):
-        refs[4 + i][...] = refs[i][...]
+    for k in range(1, SIDE):
+        y_copy(k, my_y).wait_send()
+        x_copy(k, my_x).wait_send()
+    total_all().wait_send()
+
+
+def place(out_in, ig_in, sg_in, lg_in, out, ig, sg, lg, out_v, ig_v, sg_v, lg_v, come, gone):
+    moves = [(sg_in, sg_v, sg), (lg_in, lg_v, lg)]
+    step = L // STEPS
+    for i in range(STEPS):
+        at = pl.ds(i * step, step)
+        moves.append((ig_in.at[at], ig_v.at[at], ig.at[at]))
+        moves.append((out_in.at[at], out_v.at[at], out.at[at]))
+    ins = [pltpu.make_async_copy(m[0], m[1], come.at[i]) for i, m in enumerate(moves)]
+    outs = [pltpu.make_async_copy(m[1], m[2], gone.at[i]) for i, m in enumerate(moves)]
+    for move in ins:
+        move.start()
+    for i in range(len(moves)):
+        ins[i].wait()
+        outs[i].start()
+    for move in outs:
+        move.wait()
 
 
 def body(nz, qkv, segments, short_taps, long_taps, cotangent):
@@ -509,22 +524,21 @@
             dma((CHUNKS,)), dma((CHUNKS,)), dma((CHUNKS,)), dma((CHUNKS,)), dma((CHUNKS,)), dma((CHUNKS,)),
             dma((len(SPANS),)), dma((len(SPANS),)),
             dma((len(SPANS), nz)), dma((len(SPANS), nz)),
-            dma((len(SPANS), SIDE)), dma((len(SPANS), SIDE)), dma((len(SPANS), SIDE)), dma((len(SPANS), SIDE)),
-            dma((len(SPANS),)), dma((len(SPANS),)),
+            dma((SIDE,)), dma((SIDE,)), dma((SIDE,)), dma((SIDE,)),
+            dma, dma,
         ],
         compiler_params=pltpu.CompilerParams(collective_id=0, has_side_effects=True, vmem_limit_bytes=62 * 1024 * 1024),
         cost_estimate=pl.CostEstimate(flops=20_000_000_000, bytes_accessed=10_000_000, transcendentals=0),
         name="hyena",
     )(qkv[0], segments, short_taps, long_taps, cotangent[0])
-    steps = 8
-    specs = [pl.BlockSpec((L // steps, D), lambda i: (i, 0)), pl.BlockSpec((L // steps, 3 * D), lambda i: (i, 0)),
-             pl.BlockSpec((SHORT, 3 * D // steps), lambda i: (0, i)), pl.BlockSpec((L // steps, 8 * TILES), lambda i: (i, 0))]
+    hbm = pl.BlockSpec(memory_space=pltpu.HBM)
+    moves = 2 + 2 * STEPS
     out, ig, sg, lg = pl.pallas_call(
         place,
-        grid=(steps,),
         out_shape=outs,
-        in_specs=specs,
-        out_specs=specs,
+        in_specs=[hbm] * 4,
+        out_specs=[hbm] * 4,
+        scratch_shapes=[pltpu.VMEM(o.shape, o.dtype) for o in outs] + [dma((moves,)), dma((moves,))],
         name="place",
     )(*results)
     return out[None], ig[None], sg, lg

time: 95 us -> 87 us (0.916)
  Pallas kernels: 94.1 us -> 86.3 us
    pallas_call x1, Pallas kernels: 87.5 us -> 82.1 us  [body(): pl.pallas_call(functools.partial(kernel, nz), out_shape=outs, in_specs=[p...]
    pallas_call x1, Pallas kernels: 6.65 us -> 4.14 us  [body(): pl.pallas_call(place, out_shape=outs, in_specs=[hbm] * 4, out_specs=[hbm]...]
where the time goes in v3:
time: 87 us; the launch traced here: 86.9 us
  Pallas kernels  86.3 us (99%)
    pallas_call x1, Pallas kernels, body(): pl.pallas_call(functools.partial(kernel, nz), out_shape=outs, in_specs=[p...  82.1 us
    pallas_call x1, Pallas kernels, body(): pl.pallas_call(place, out_shape=outs, in_specs=[hbm] * 4, out_specs=[hbm]...  4.14 us

profile of v3, /device:TPU:1, one launch (start us, length us, event | category | flops | bytes accessed | tf_op | source)
XLA Modules:
  0.0 86.9 jit_solution(1926146681351263237)
XLA Ops:
  0.6 82.1 %hyena.1 = (bf16[128,4096]{1,0:T(8,128)(2,1)}, bf16[128,12288]{1,0:T(8,128)(2,1)}, f32[7,12288]{1,0:T(8,128)}, f32[128,256]{1,0:T(8,128)}) custom-call(bf16[128,12288]{1,0:T(8,128)(2,1)} %bitcast.4, s32[1,2048]{1,0:T(1,128)} %segs_hbm.1, f32[7,12288]{1,0:T(8,128)} %staps_hbm.1, bf16[128,256]{1,0:T(8,128)(2,1)} %ltaps_hbm.1, bf16[128,4096]{1,0:T(8,128)(2,1)} %bitcast.6), custom_call_target="tpu_custom_call" | custom-call | flops 20000000000 | bytes 10000000 | tf_op jit(solution)/shard_map/hyena/pallas_call | solution.py:482
  82.8 4.1 %place.1 = (bf16[128,4096]{1,0:T(8,128)(2,1)}, bf16[128,12288]{1,0:T(8,128)(2,1)}, f32[7,12288]{1,0:T(8,128)}, f32[128,256]{1,0:T(8,128)}) custom-call(bf16[128,4096]{1,0:T(8,128)(2,1)} %get-tuple-element.12.out_in, bf16[128,12288]{1,0:T(8,128)(2,1)} %get-tuple-element.13.ig_in, f32[7,12288]{1,0:T(8,128)} %get-tuple-element.14.sg_in, ...), custom_call_target="tpu_custom_call" | custom-call | tf_op jit(solution)/shard_map/place/pallas_call | solution.py:536

commit v4 on v3

--- a/solution.py
+++ b/solution.py
@@ -21,9 +21,10 @@
 SPANS = ((0, 4), (4, 4))
 LOOP_STAGES = ((11, "a", 0), (14, "b", 0))
 STEPS = 4
-PART = 4
-EARLY = 8
-AHEAD = 3
+PART = 2
+READY = 2
+EARLY = 4
+AHEAD = 4
 ROWS = 16
 LAG = 4
 F32 = jnp.float32
@@ -180,13 +181,19 @@
 
     lax.fori_loop(0, EARLY, first, 0)
     pl.semaphore_wait(barrier, ndp - 1 + 2 + 2 * (SIDE - 1))
-    for i in range(CHUNKS // PART):
+    parts = CHUNKS // PART
+    for i in range(READY):
         hq_copy(i).start()
     for c in range(AHEAD):
         gg_copy(c).start()
-    lax.fori_loop(EARLY, CHUNKS, first, 0)
-    for c in range(AHEAD):
-        prod_copy(c).start()
+    middle = (EARLY + CHUNKS) // 2
+    lax.fori_loop(EARLY, middle, first, 0)
+    for i in range(READY, 2 * READY):
+        hq_copy(i).start()
+    prod_copy(0).start()
+    lax.fori_loop(middle, CHUNKS, first, 0)
+    for i in range(2 * READY, parts):
+        hq_copy(i).start()
 
     def first_rows(c, carry):
         halos = unpack(hq_in, c)
@@ -212,7 +219,9 @@
         gg_head(i).start()
         return carry
 
-    lax.fori_loop(0, CHUNKS // PART, first_part, 0)
+    lax.fori_loop(0, READY, first_part, 0)
+    for c in range(1, AHEAD):
+        prod_copy(c).start()
 
     def second(c):
         parts = []
@@ -358,6 +367,10 @@
         lax.fori_loop(1, ndp, step, 0)
 
     def take(c):
+        @pl.when(jnp.logical_and(lax.rem(c, PART) == 0, c // PART + READY < parts))
+        def _():
+            first_part(c // PART + READY, 0)
+
         @pl.when(lax.rem(c, PART) == 0)
         def _():
             prod_head(c // PART).wait_recv()

time: 87 us -> 83.6 us (0.961)
  Pallas kernels: 86.3 us -> 82.8 us
    pallas_call x1, Pallas kernels: 82.1 us -> 78.6 us  [body(): pl.pallas_call(functools.partial(kernel, nz), out_shape=outs, in_specs=[p...]
where the time goes in v4:
time: 83.6 us; the launch traced here: 83.4 us
  Pallas kernels  82.8 us (99%)
    pallas_call x1, Pallas kernels, body(): pl.pallas_call(functools.partial(kernel, nz), out_shape=outs, in_specs=[p...  78.6 us
    pallas_call x1, Pallas kernels, body(): pl.pallas_call(place, out_shape=outs, in_specs=[hbm] * 4, out_specs=[hbm]...  4.14 us

profile of v4, /device:TPU:1, one launch (start us, length us, event | category | flops | bytes accessed | tf_op | source)
XLA Modules:
  0.0 83.4 jit_solution(5527589089568662587)
XLA Ops:
  0.6 78.6 %hyena.1 = (bf16[128,4096]{1,0:T(8,128)(2,1)}, bf16[128,12288]{1,0:T(8,128)(2,1)}, f32[7,12288]{1,0:T(8,128)}, f32[128,256]{1,0:T(8,128)}) custom-call(bf16[128,12288]{1,0:T(8,128)(2,1)} %bitcast.4, s32[1,2048]{1,0:T(1,128)} %segs_hbm.1, f32[7,12288]{1,0:T(8,128)} %staps_hbm.1, bf16[128,256]{1,0:T(8,128)(2,1)} %ltaps_hbm.1, bf16[128,4096]{1,0:T(8,128)(2,1)} %bitcast.6), custom_call_target="tpu_custom_call" | custom-call | flops 20000000000 | bytes 10000000 | tf_op jit(solution)/shard_map/hyena/pallas_call | solution.py:495
  79.3 4.1 %place.1 = (bf16[128,4096]{1,0:T(8,128)(2,1)}, bf16[128,12288]{1,0:T(8,128)(2,1)}, f32[7,12288]{1,0:T(8,128)}, f32[128,256]{1,0:T(8,128)}) custom-call(bf16[128,4096]{1,0:T(8,128)(2,1)} %get-tuple-element.12.out_in, bf16[128,12288]{1,0:T(8,128)(2,1)} %get-tuple-element.13.ig_in, f32[7,12288]{1,0:T(8,128)} %get-tuple-element.14.sg_in, ...), custom_call_target="tpu_custom_call" | custom-call | tf_op jit(solution)/shard_map/place/pallas_call | solution.py:549
